TPU v7x, 256 devices: a whole 4x4x8 slice. The times are simulated.
256 devices in a mesh: blk: 64 (over y_hi, x, z), head: 4 (over y_lo, core).
Axes of the slice: x: 4, y: 4 (y_hi: 2, y_lo: 2; y = y_hi * 2 + y_lo), z: 8, core: 2. Of those that a mesh axis runs over, the one named last changes fastest.
Arguments:
- img_q: bfloat16 [32768, 3072], P(('blk', 'head')), may hold values from -60 to 60
- img_k: bfloat16 [32768, 3072], P(('blk', 'head')), may hold values from -20 to 20
- img_v: bfloat16 [32768, 3072], P(('blk', 'head')), may hold values from -6 to 6
- img_grad: bfloat16 [32768, 3072], P(('blk', 'head')), may hold values from -6 to 6
- txt_q: bfloat16 [256, 3072], P(None, 'head'), may hold values from -60 to 60
- txt_k: bfloat16 [256, 3072], P(None, 'head'), may hold values from -20 to 20
- txt_v: bfloat16 [256, 3072], P(None, 'head'), may hold values from -6 to 6
- txt_grad: bfloat16 [256, 3072], P(None, 'head'), may hold values from -6 to 6
Outputs:
- grad_img_q: bfloat16 [32768, 3072], P(('blk', 'head'))
- grad_img_k: bfloat16 [32768, 3072], P(('blk', 'head'))
- grad_img_v: bfloat16 [32768, 3072], P(('blk', 'head'))
- grad_txt_q: float32 [256, 3072], P(None, 'head')
- grad_txt_k: float32 [256, 3072], P(None, 'head')
- grad_txt_v: float32 [256, 3072], P(None, 'head')
All inputs are finite; a program needn't handle non-finite values.
Results may differ from a plain program's by a relative error of at most 0.006.
Values may be sent and summed in bfloat16 or wider, within the bound.
A program may use at most 192 MiB of HBM per device.

v0:
```python
import jax
import jax.numpy as jnp
from jax import lax
from jax.sharding import PartitionSpec as P

HEAD_DIM = 128


def shifted(array, axis, by):
    peers = lax.axis_size(axis)
    return lax.ppermute(array, axis, [(i, (i + by) % peers) for i in range(peers)])


def heads_first(matrix):
    return matrix.reshape(matrix.shape[0], -1, HEAD_DIM).transpose(1, 0, 2)


def heads_last(stack):
    return stack.transpose(1, 0, 2).reshape(stack.shape[1], -1)


def cross_dot(left, right):
    return lax.dot_general(
        left, right, (((1,), (1,)), ((), ())), preferred_element_type=jnp.float32
    )


def tall_dot(left, right):
    return lax.dot_general(
        left, right, (((0,), (0,)), ((), ())), preferred_element_type=jnp.float32
    )


def partial_stats(scores, dprobs):
    row_top = jnp.max(scores, axis=1)
    lifted = jnp.exp(scores - row_top[:, None])
    return (row_top, jnp.sum(lifted, axis=1), jnp.sum(lifted * dprobs, axis=1))


def row_grads(scores, dprobs, row_top, row_total, row_delta, queries, grads, all_keys, scaling):
    weights = jnp.exp(scores - row_top[:, None]) / row_total[:, None]
    dscore = (weights * (dprobs - row_delta[:, None])).astype(jnp.bfloat16)
    probs_bf = weights.astype(jnp.bfloat16)
    grad_query = jnp.dot(dscore, all_keys, preferred_element_type=jnp.float32) * scaling
    grad_key = tall_dot(dscore, queries) * scaling
    grad_value = tall_dot(probs_bf, grads)
    return (grad_query, grad_key, grad_value)


def body(img_q, img_k, img_v, img_grad, txt_q, txt_k, txt_v, txt_grad):
    scaling = HEAD_DIM ** (-0.5)
    query_rows, key_rows, value_rows, grad_rows = (
        lax.all_to_all(img_q, "head", split_axis=1, concat_axis=0, tiled=True),
        lax.all_to_all(img_k, "head", split_axis=1, concat_axis=0, tiled=True),
        lax.all_to_all(img_v, "head", split_axis=1, concat_axis=0, tiled=True),
        lax.all_to_all(img_grad, "head", split_axis=1, concat_axis=0, tiled=True),
    )
    row_count = query_rows.shape[0]
    query_heads = heads_first(query_rows)
    key_heads = heads_first(key_rows)
    value_heads = heads_first(value_rows)
    grad_heads = heads_first(grad_rows)
    text_query = heads_first(txt_q)
    text_key = heads_first(txt_k)
    text_value = heads_first(txt_v)
    text_grad = heads_first(txt_grad)
    text_scores = (
        jnp.einsum("hqd,hkd->hqk", text_query, key_heads, preferred_element_type=jnp.float32)
        * scaling
    )
    self_scores = (
        jnp.einsum("hqd,hkd->hqk", text_query, text_key, preferred_element_type=jnp.float32)
        * scaling
    )
    text_dprobs = jnp.einsum(
        "hqd,hkd->hqk", text_grad, value_heads, preferred_element_type=jnp.float32
    )
    self_dprobs = jnp.einsum(
        "hqd,hkd->hqk", text_grad, text_value, preferred_element_type=jnp.float32
    )
    local_top = jnp.maximum(jnp.max(text_scores, axis=-1), jnp.max(self_scores, axis=-1))
    joint = lax.pmax(local_top, "blk")
    lifted_text = jnp.exp(text_scores - joint[..., None])
    totals, dot_sums = lax.psum(
        (jnp.sum(lifted_text, axis=-1), jnp.sum(lifted_text * text_dprobs, axis=-1)), "blk"
    )
    lifted_self = jnp.exp(self_scores - joint[..., None])
    row_total = totals + jnp.sum(lifted_self, axis=-1)
    row_delta = (dot_sums + jnp.sum(lifted_self * self_dprobs, axis=-1)) / row_total
    text_weights = jnp.exp(text_scores - joint[..., None]) / row_total[..., None]
    self_weights = jnp.exp(self_scores - joint[..., None]) / row_total[..., None]
    text_dscore = (text_weights * (text_dprobs - row_delta[..., None])).astype(jnp.bfloat16)
    self_dscore = (self_weights * (self_dprobs - row_delta[..., None])).astype(jnp.bfloat16)
    text_probs_bf = text_weights.astype(jnp.bfloat16)
    self_probs_bf = self_weights.astype(jnp.bfloat16)
    text_query_part = (
        jnp.einsum("hqk,hkd->hqd", text_dscore, key_heads, preferred_element_type=jnp.float32)
        * scaling
    )
    key_from_text = (
        jnp.einsum("hqk,hqd->hkd", text_dscore, text_query, preferred_element_type=jnp.float32)
        * scaling
    )
    value_from_text = jnp.einsum(
        "hqk,hqd->hkd", text_probs_bf, text_grad, preferred_element_type=jnp.float32
    )
    self_query = (
        jnp.einsum("hqk,hkd->hqd", self_dscore, text_key, preferred_element_type=jnp.float32)
        * scaling
    )
    self_key = (
        jnp.einsum("hqk,hqd->hkd", self_dscore, text_query, preferred_element_type=jnp.float32)
        * scaling
    )
    self_value = jnp.einsum(
        "hqk,hqd->hkd", self_probs_bf, text_grad, preferred_element_type=jnp.float32
    )
    prev_keys, prev_values = shifted((key_rows, value_rows), "blk", 1)

    def one_head(pieces):
        query_h, grad_h, key_h, value_h, prev_key, prev_value, text_key_h, text_value_h = pieces
        all_keys = jnp.concatenate([key_h, prev_key, text_key_h], axis=0)
        all_values = jnp.concatenate([value_h, prev_value, text_value_h], axis=0)
        scores = cross_dot(query_h, all_keys) * scaling
        dprobs = cross_dot(grad_h, all_values)
        row_top, row_sum, dot_total = partial_stats(scores, dprobs)
        return row_grads(
            scores,
            dprobs,
            row_top,
            row_sum,
            dot_total / row_sum,
            query_h,
            grad_h,
            all_keys,
            scaling,
        )

    grad_query, grad_key, grad_value = lax.map(
        one_head,
        (
            query_heads,
            grad_heads,
            key_heads,
            value_heads,
            heads_first(prev_keys),
            heads_first(prev_values),
            text_key,
            text_value,
        ),
    )
    back_key, back_value = shifted(
        (
            heads_last(grad_key[:, row_count : 2 * row_count]),
            heads_last(grad_value[:, row_count : 2 * row_count]),
        ),
        "blk",
        -1,
    )
    image_query = heads_last(grad_query)
    image_key = heads_last(grad_key[:, :row_count] + key_from_text) + back_key
    image_value = heads_last(grad_value[:, :row_count] + value_from_text) + back_value
    text_key_part = grad_key[:, 2 * row_count :]
    text_value_part = grad_value[:, 2 * row_count :]
    summed_query, summed_key, summed_value = lax.psum(
        (heads_last(text_query_part), heads_last(text_key_part), heads_last(text_value_part)), "blk"
    )
    out_query, out_key, out_value = (
        lax.all_to_all(
            image_query.astype(jnp.bfloat16), "head", split_axis=0, concat_axis=1, tiled=True
        ),
        lax.all_to_all(
            image_key.astype(jnp.bfloat16), "head", split_axis=0, concat_axis=1, tiled=True
        ),
        lax.all_to_all(
            image_value.astype(jnp.bfloat16), "head", split_axis=0, concat_axis=1, tiled=True
        ),
    )
    return (
        out_query,
        out_key,
        out_value,
        summed_query + heads_last(self_query),
        summed_key + heads_last(self_key),
        summed_value + heads_last(self_value),
    )


def solution(mesh):
    return jax.shard_map(
        body,
        mesh=mesh,
        in_specs=(
            P(("blk", "head"), None),
            P(("blk", "head"), None),
            P(("blk", "head"), None),
            P(("blk", "head"), None),
            P(None, "head"),
            P(None, "head"),
            P(None, "head"),
            P(None, "head"),
        ),
        out_specs=(
            P(("blk", "head"), None),
            P(("blk", "head"), None),
            P(("blk", "head"), None),
            P(None, "head"),
            P(None, "head"),
            P(None, "head"),
        ),
        check_vma=False,
    )
```

profile of v0, /device:TPU:24, one launch (start us, length us, event | category | flops | bytes accessed | tf_op | source)
XLA Modules:
  0.0 1485.1 jit_solution(12469456330407125909)
XLA Ops:
  9.5 4.3 all-to-all-start
  15.0 8.8 all-to-all-done
  23.9 5.1 all-to-all-start.1
  30.2 8.8 all-to-all-done.1
  39.0 5.1 all-to-all-start.3
  45.3 8.8 all-to-all-done.3
  54.1 5.1 all-to-all-start.2
  65.4 2.6 fusion.50
  85.5 204.0 %pmax.7 = f32[6,256]{1,0:T(8,128)S(1)} all-reduce(f32[6,256]{1,0:T(8,128)S(1)} %max.5), channel_id=1, replica_groups=mesh['blk'=64,'head'=4] {'blk'}, use_global_device_ids=true, to_apply=%region_7.0 | all-reduce | flops 1536 | bytes 12288 | tf_op jit(solution)/shard_map/pmax | solution.py:82
  289.5 4.7 multiply_reduce_fusion.1
  294.2 351.9 %all-reduce = (f32[6,256]{1,0:T(8,128)S(1)}, f32[6,256]{1,0:T(8,128)S(1)}) all-reduce(f32[6,256]{1,0:T(8,128)} %get-tuple-element.130, f32[6,256]{1,0:T(8,128)S(1)} %get-tuple-element.129), channel_id=1, replica_groups=mesh['blk'=64,'head'=4] {'blk'}, use_global_device_ids=true, to_apply=%region_9.10 | all-reduce | flops 3072 | bytes 24576 | tf_op jit(solution)/shard_map/psum | solution.py:84
  646.1 3.1 multiply_reduce_fusion.3
  653.9 93.2 %while.14 = (s32[]{:T(128)}, bf16[6,512,128]{2,1,0:T(8,128)(2,1)}, f32[6,1280,128]{1,2,0:T(8,128)}, f32[6,1280,128]{1,2,0:T(8,128)}, bf16[6,512,128]{1,2,0:T(8,1...) while((s32[]{:T(128)}, bf16[6,512,128]{2,1,0:T(8,128)(2,1)}, ...), condition=%wide.region_4.0_spmd, body=%wide.region_0.4_spmd.sunk | while | flops 851213312 | bytes 27485348 | solution.py:139
  667.0 2.5 fusion.89
  682.5 2.5 fusion.89
  698.1 2.5 fusion.89
  713.6 2.5 fusion.89
  729.1 2.5 fusion.89
  744.7 2.5 fusion.89
  747.1 2.9 slice.19
  750.1 2.5 multiply_convert_fusion.1
  755.7 3.1 slice.21
  767.9 2.5 convert_element_type.36
  772.5 4.2 all-to-all-start.4
  776.7 3.4 multiply_add_fusion
  787.5 4.8 all-to-all-start.5
  792.3 2.5 slice_add_fusion
  797.6 5.4 all-to-all-done.5
  802.9 5.8 all-to-all-start.6
  810.5 2.4 copy.169
  815.1 4.4 all-to-all-done.6
  821.8 651.7 %all-reduce.4.cloned.1.call-done = (f32[256,768]{1,0:T(8,128)}, f32[256,768]{0,1:T(8,128)}, f32[256,768]{0,1:T(8,128)}) async-done(((f32[256,768]{1,0:T(8,128)}, f32[256,768]{0,1:T(8,128)}, f32[256,768]{0,1:T(8,128)}), (f32[256,768]{1,0:T(8,128)}, f32[256,768]{0,1:T(8,128)}, f32[256,768]{0,1:T(8,128)})) %all-reduce.4.cloned.1.call-update) | async-done | bytes 2359312 | tf_op jit(solution)/shard_map/psum | solution.py:165
  (197 shorter events, 147.7 us)
Async XLA Ops:
  7.2 6.7 copy-start.18
  9.5 19.5 %copy-start.19 = (bf16[128,3072]{1,0:T(8,128)(2,1)S(1)}, bf16[128,3072]{1,0:T(8,128)(2,1)}, u32[]{:S(2)}) copy-start(bf16[128,3072]{1,0:T(8,128)(2,1)} %param.12) | copy-start | bytes 2359300
  9.5 14.3 all-to-all-start
  15.0 29.1 %copy-start.20 = (bf16[128,3072]{1,0:T(8,128)(2,1)S(1)}, bf16[128,3072]{1,0:T(8,128)(2,1)}, u32[]{:S(2)}) copy-start(bf16[128,3072]{1,0:T(8,128)(2,1)} %param.13) | copy-start | bytes 2359300
  23.9 15.1 %all-to-all-start.1 = ((bf16[128,4,768]{0,2,1:T(8,128)(2,1)}), bf16[128,4,768]{0,2,1:T(8,128)(2,1)S(1)}, u32[]{:S(2)}, u32[]{:S(2)}) async-start(bf16[128,4,768]{0,2,1:T(8,128)(2,1)} %bitcast.14), calls=%async_computation.1 | async-start | bytes 1572864 | tf_op jit(solution)/shard_map/all_to_all | solution.py:54
  30.2 29.1 %copy-start.22 = (bf16[256,768]{1,0:T(8,128)(2,1)S(1)}, bf16[256,768]{1,0:T(8,128)(2,1)}, u32[]{:S(2)}) copy-start(bf16[256,768]{1,0:T(8,128)(2,1)} %param.15) | copy-start | bytes 1179652
  39.0 15.1 %all-to-all-start.3 = ((bf16[128,4,768]{0,2,1:T(8,128)(2,1)}), bf16[128,4,768]{0,2,1:T(8,128)(2,1)S(1)}, u32[]{:S(2)}, u32[]{:S(2)}) async-start(bf16[128,4,768]{0,2,1:T(8,128)(2,1)} %bitcast.25), calls=%async_computation.3 | async-start | bytes 1572864 | tf_op jit(solution)/shard_map/all_to_all | solution.py:55
  54.1 24.3 %all-to-all-start.2 = ((bf16[128,4,768]{0,2,1:T(8,128)(2,1)}), bf16[128,4,768]{0,2,1:T(8,128)(2,1)S(1)}, u32[]{:S(2)}, u32[]{:S(2)}) async-start(bf16[128,4,768]{0,2,1:T(8,128)(2,1)} %bitcast.22), calls=%async_computation.2 | async-start | bytes 1572864 | tf_op jit(solution)/shard_map/all_to_all | solution.py:56
  63.3 20.4 %copy-start.5 = (bf16[256,768]{0,1:T(8,128)(2,1)}, bf16[256,768]{0,1:T(8,128)(2,1)S(1)}, u32[]{:S(2)}) copy-start(bf16[256,768]{0,1:T(8,128)(2,1)S(1)} %copy.148) | copy-start | bytes 1179652
  75.4 5.2 copy-start.7
  75.4 4.9 copy-start.15
  76.5 572.7 %collective-permute-start = (bf16[512,768]{1,0:T(8,128)(2,1)}, bf16[512,768]{1,0:T(8,128)(2,1)}, u32[]{:S(2)}, u32[]{:S(2)}) collective-permute-start(bf16[512,768]{1,0:T(8,128)(2,1)} %bitcast.17), channel_id=1, source_target_pairs={{0,4},{4,8},{8,12},{12,16},{16,20},{20,24},{24,28},{28,32},{32,36}... | collective-permute-start | bytes 2359304 | tf_op jit(solution)/shard_map/ppermute | solution.py:11
  81.7 569.9 %collective-permute-start.1 = (bf16[512,768]{1,0:T(8,128)(2,1)}, bf16[512,768]{1,0:T(8,128)(2,1)}, u32[]{:S(2)}, u32[]{:S(2)}) collective-permute-start(bf16[512,768]{1,0:T(8,128)(2,1)} %bitcast.28), channel_id=1, source_target_pairs={{0,4},{4,8},{8,12},{12,16},{16,20},{20,24},{24,28},{28,32},{32,36}... | collective-permute-start | bytes 2359304 | tf_op jit(solution)/shard_map/ppermute | solution.py:11
  85.5 208.8 %copy-start = (f32[6,256,512]{2,1,0:T(8,128)}, f32[6,256,512]{2,1,0:T(8,128)S(1)}, u32[]{:S(2)}) copy-start(f32[6,256,512]{2,1,0:T(8,128)S(1)} %get-tuple-element.174) | copy-start | bytes 9437188
  289.5 356.6 %copy-start.12 = (bf16[256,768]{0,1:T(8,128)(2,1)S(1)}, bf16[256,768]{0,1:T(8,128)(2,1)}, u32[]{:S(2)}) copy-start(bf16[256,768]{0,1:T(8,128)(2,1)} %copy.152) | copy-start | bytes 1179652
  747.1 2.9 copy-start.1
  750.1 34.3 %collective-permute-start.2 = (f32[512,768]{0,1:T(8,128)}, f32[512,768]{0,1:T(8,128)}, u32[]{:S(2)}, u32[]{:S(2)}) collective-permute-start(f32[512,768]{0,1:T(8,128)} %bitcast.47), channel_id=1, source_target_pairs={{0,252},{4,0},{8,4},{12,8},{16,12},{20,16},{24,20},{28,24},{32,28}... | collective-permute-start | bytes 4718600 | tf_op jit(solution)/shard_map/ppermute | solution.py:11
  750.1 2.5 copy-start.8
  752.6 3.1 copy-start.4
  752.6 2.7 copy-start.11
  755.7 3.1 copy-start.9
  758.8 36.0 %collective-permute-start.3 = (f32[512,768]{0,1:T(8,128)}, f32[512,768]{0,1:T(8,128)}, u32[]{:S(2)}, u32[]{:S(2)}) collective-permute-start(f32[512,768]{0,1:T(8,128)} %bitcast.53), channel_id=1, source_target_pairs={{0,252},{4,0},{8,4},{12,8},{16,12},{20,16},{24,20},{28,24},{32,28}... | collective-permute-start | bytes 4718600 | tf_op jit(solution)/shard_map/ppermute | solution.py:11
  767.8 8.8 copy-start.6
  772.5 15.1 %all-to-all-start.4 = ((bf16[4,128,768]{1,2,0:T(8,128)(2,1)}), bf16[4,128,768]{1,2,0:T(8,128)(2,1)}, u32[]{:S(2)}, u32[]{:S(2)}) async-start(bf16[4,128,768]{1,2,0:T(8,128)(2,1)} %copy.146), calls=%async_computation.4 | async-start | bytes 1572864 | tf_op jit(solution)/shard_map/all_to_all | solution.py:169
  776.6 696.8 %all-reduce.4.cloned.1.call-start = ((), (), s32[]{:S(2)}) async-start(), calls=%async_computation.7 | async-start | bytes 4718592 | tf_op jit(solution)/shard_map/psum | solution.py:165
  787.5 15.4 %all-to-all-start.5 = ((bf16[4,128,768]{1,2,0:T(8,128)(2,1)}), bf16[4,128,768]{1,2,0:T(8,128)(2,1)}, u32[]{:S(2)}, u32[]{:S(2)}) async-start(bf16[4,128,768]{1,2,0:T(8,128)(2,1)} %copy_bitcast_fusion.1), calls=%async_computation.5 | async-start | bytes 1572864 | tf_op jit(solution)/shard_map/all_to_all | solution.py:172
  794.8 14.0 copy-start.10
  796.5 13.5 copy-start.3
  796.5 13.5 copy-start.13
  802.9 16.6 %all-to-all-start.6 = ((bf16[4,128,768]{1,2,0:T(8,128)(2,1)}), bf16[4,128,768]{1,2,0:T(8,128)(2,1)}, u32[]{:S(2)}, u32[]{:S(2)}) async-start(bf16[4,128,768]{1,2,0:T(8,128)(2,1)} %copy_bitcast_fusion), calls=%async_computation.6 | async-start | bytes 1572864 | tf_op jit(solution)/shard_map/all_to_all | solution.py:175
  810.5 663.0 %copy-start.14 = (f32[6,256,128]{1,2,0:T(8,128)S(1)}, f32[6,256,128]{1,2,0:T(8,128)}, u32[]{:S(2)}) copy-start(f32[6,256,128]{1,2,0:T(8,128)} %convolution_multiply_fusion.5) | copy-start | bytes 2359300
  1475.0 2.3 copy-start.17
  (3 other events, 6.4 us)
Sparse Core Ops, SparseCore 0:
  784.5 688.9 all-reduce.3
where the time goes:
time: 1490 us
  waiting for transfers between devices  688 us (46%)
  blocking collectives  556 us (37%)
  local copies, waits for them, and re-layouts  101 us (7%)
  matrix products  74.1 us (5%)
  starting transfers between devices  38.4 us (3%)
    psum x1, waiting for transfers between devices, body(): lax.psum((heads_last(text_query_part), heads_last(text_key_part), heads_l...  652 us
    psum x1, blocking collectives, body(): lax.psum((jnp.sum(lifted_text, axis=-1), jnp.sum(lifted_text * text_dprob...  352 us
    pmax x1, blocking collectives, body(): joint = lax.pmax(local_top, 'blk')  204 us
  transfers between devices with their start and end apart: 12, of which 6 were waited for; matrix products, arithmetic and copies ran while one was open for 5% of the time, Pallas kernels for 0%

commit v1 on v0

v1 whole, which is shorter than its diff:
```python
import functools
import math

import jax
import jax.numpy as jnp
from jax import lax
from jax.experimental import pallas as pl
from jax.experimental.pallas import tpu as pltpu
from jax.sharding import PartitionSpec as P

HEAD_DIM = 128
SCALE = HEAD_DIM ** (-0.5)
EXP2_SCALE = SCALE * math.log2(math.e)
MESH = pl.DeviceIdType.MESH
F32 = jnp.float32
BF16 = jnp.bfloat16
STAT_ROWS = 8
VMEM_LIMIT = 50 * 1024 * 1024


def torus_sizes(blocks):
    return {64: (2, 4, 8), 8: (2, 2, 2), 4: (1, 2, 2)}[blocks]


class Place:
    def __init__(self, blocks, heads):
        self.blocks, self.heads = blocks, heads
        self.n_hi, self.n_x, self.n_z = torus_sizes(blocks)
        self.b = lax.axis_index("blk")
        self.c = lax.axis_index("head")
        self.z = lax.rem(self.b, self.n_z)
        self.x = lax.rem(self.b // self.n_z, self.n_x)
        self.hi = self.b // (self.n_z * self.n_x)

    def device(self, hi, x, z):
        return ((hi * self.n_x + x) * self.n_z + z, self.c)

    def next(self):
        return (lax.rem(self.b + 1, self.blocks), self.c)

    def prev(self):
        return (lax.rem(self.b + self.blocks - 1, self.blocks), self.c)

    def head_peer(self, step):
        return lax.rem(self.c + step, self.heads)

    def along_z(self, step):
        z = lax.rem(self.z + step, self.n_z)
        return z, self.device(self.hi, self.x, z)

    def along_x(self, step):
        x = lax.rem(self.x + step, self.n_x)
        return x, self.device(self.hi, x, self.z)

    def along_hi(self, step):
        return self.device(lax.rem(self.hi + step, self.n_hi), self.x, self.z)

    def in_plane(self, step):
        at = lax.rem(self.hi * self.n_x + self.x + step, self.n_hi * self.n_x)
        return self.device(at // self.n_x, lax.rem(at, self.n_x), self.z)


def meet(devices):
    barrier = pltpu.get_barrier_semaphore()
    for device in devices:
        pl.semaphore_signal(barrier, inc=1, device_id=device, device_id_type=MESH)
    pl.semaphore_wait(barrier, len(devices))


def remote(src, dst, sems, slot, device):
    return pltpu.make_async_remote_copy(
        src_ref=src,
        dst_ref=dst,
        send_sem=sems.at[(0,) + slot],
        recv_sem=sems.at[(1,) + slot],
        device_id=device,
        device_id_type=MESH,
    )


def dot_last(left, right):
    return lax.dot_general(
        left, right, (((1,), (1,)), ((), ())), preferred_element_type=F32
    )


def dot_plain(left, right):
    return lax.dot_general(
        left, right, (((1,), (0,)), ((), ())), preferred_element_type=F32
    )


def col_max(array):
    return jnp.max(array, axis=0, keepdims=True)


def col_sum(array):
    return jnp.sum(array, axis=0, keepdims=True)


def merge_stats(parts):
    top = functools.reduce(jnp.maximum, [p[0] for p in parts])
    total = jnp.zeros_like(top)
    dots = jnp.zeros_like(top)
    for part_top, part_total, part_dots in parts:
        factor = jnp.exp2(part_top - top)
        total += part_total * factor
        dots += part_dots * factor
    return top, total, dots


def split_stats(array):
    return tuple(array[i * STAT_ROWS : (i + 1) * STAT_ROWS] for i in range(3))


def gather_kernel(
    blocks, heads, img_q, img_k, img_v, img_g, txt_q, txt_k, txt_v, txt_g,
    q_all, k_all, v_all, g_all, k_prev, v_prev, stats,
    stat_z, stat_p, a2a_sems, own_sems, halo_sems, z_sems, p_sems,
):
    at = Place(blocks, heads)
    rows = img_q.shape[0]
    wide = q_all.shape[1]
    per_dev = wide // HEAD_DIM
    n_plane = at.n_hi * at.n_x
    meet(
        [(at.b, at.head_peer(s)) for s in range(1, heads)]
        + [at.next(), at.prev()]
        + [at.along_z(s)[1] for s in range(1, at.n_z)]
        + [at.in_plane(s) for s in range(1, n_plane)]
    )
    my_rows = pl.ds(at.c * rows, rows)
    arrays = [(img_k, k_all), (img_v, v_all), (img_q, q_all), (img_g, g_all)]
    sends = []
    for i, (src, dst) in enumerate(arrays):
        for s in range(1, heads):
            peer = at.head_peer(s)
            copy = remote(
                src.at[:, pl.ds(peer * wide, wide)],
                dst.at[my_rows, :],
                a2a_sems,
                (i, s),
                (at.b, peer),
            )
            copy.start()
            sends.append((i, copy))
        own = pltpu.make_async_copy(
            src.at[:, pl.ds(at.c * wide, wide)], dst.at[my_rows, :], own_sems.at[i]
        )
        own.start()
        sends.append((i, own))
    halo = []
    for i, dst in enumerate((k_prev, v_prev)):
        for j, copy in sends:
            if i == j:
                copy.wait()
        copy = remote(arrays[i][1], dst, halo_sems, (i,), at.next())
        copy.start()
        halo.append(copy)
    first = jnp.where(at.b == 0, 1.0, 0.0).astype(F32)
    stats[...] = jnp.zeros_like(stats)
    for h in range(per_dev):
        cols = pl.ds(h * HEAD_DIM, HEAD_DIM)
        query, grad = txt_q[:, cols], txt_g[:, cols]
        s_img = dot_last(k_all[:, cols], query) * EXP2_SCALE
        s_txt = dot_last(txt_k[:, cols], query) * EXP2_SCALE
        top = jnp.maximum(col_max(s_img), col_max(s_txt))
        p_img = jnp.exp2(s_img - top)
        p_txt = jnp.exp2(s_txt - top) * first
        d_img = dot_last(v_all[:, cols], grad)
        d_txt = dot_last(txt_v[:, cols], grad)
        stats[h : h + 1, :] = top
        stats[STAT_ROWS + h : STAT_ROWS + h + 1, :] = col_sum(p_img) + col_sum(p_txt)
        stats[2 * STAT_ROWS + h : 2 * STAT_ROWS + h + 1, :] = (
            col_sum(p_img * d_img) + col_sum(p_txt * d_txt)
        )
    stat_z[0] = stats[...]
    copies = []
    for s in range(1, at.n_z):
        copy = remote(stat_z.at[0], stat_z.at[s], z_sems, (s,), at.along_z(s)[1])
        copy.start()
        copies.append(copy)
    for copy in copies:
        copy.wait()
    merged = merge_stats([split_stats(stat_z[s]) for s in range(at.n_z)])
    for i in range(3):
        stat_p[0, i * STAT_ROWS : (i + 1) * STAT_ROWS, :] = merged[i]
    copies = []
    for s in range(1, n_plane):
        copy = remote(stat_p.at[0], stat_p.at[s], p_sems, (s,), at.in_plane(s))
        copy.start()
        copies.append(copy)
    for copy in copies:
        copy.wait()
    merged = merge_stats([split_stats(stat_p[s]) for s in range(n_plane)])
    for i in range(3):
        stats[i * STAT_ROWS : (i + 1) * STAT_ROWS, :] = merged[i]
    for copy in halo:
        copy.wait()
    for i, copy in sends:
        if i >= 2:
            copy.wait()


def attention_kernel(
    blocks, q, k, v, g, kp, vp, tq, tk, tv, tg, stats,
    dq, dko, dvo, dkp, dvp, dtq, dtk, dtv,
):
    h = pl.program_id(0)
    first = jnp.where(lax.axis_index("blk") == 0, 1.0, 0.0).astype(F32)
    query, grad = tq[...], tg[...]
    top = stats[pl.ds(h, 1), :]
    total = stats[pl.ds(STAT_ROWS + h, 1), :]
    delta = stats[pl.ds(2 * STAT_ROWS + h, 1), :] / total
    inverse = 1.0 / total
    w_img = jnp.exp2(dot_last(k[...], query) * EXP2_SCALE - top) * inverse
    ds_img = (w_img * (dot_last(v[...], grad) - delta)).astype(BF16)
    w_txt = jnp.exp2(dot_last(tk[...], query) * EXP2_SCALE - top) * (inverse * first)
    ds_txt = (w_txt * (dot_last(tv[...], grad) - delta)).astype(BF16)
    k_t, tk_t = k[...].T, tk[...].T
    dtq[...] = (dot_plain(k_t, ds_img) + dot_plain(tk_t, ds_txt)).T * SCALE
    dko[...] = dot_plain(ds_img, query)
    dvo[...] = dot_plain(w_img.astype(BF16), grad)
    dtk[...] = dot_plain(ds_txt, query)
    dtv[...] = dot_plain(w_txt.astype(BF16), grad)
    kp_t = kp[...].T
    keys = [k, kp, tk]
    values = [v, vp, tv]
    tile = 256
    dk_parts, dv_parts = [None] * 3, [None] * 3
    for r in range(0, q.shape[0], tile):
        query, grad = q[r : r + tile, :], g[r : r + tile, :]
        scores = [dot_last(key[...], query) for key in keys]
        top = functools.reduce(jnp.maximum, [col_max(s) for s in scores]) * EXP2_SCALE
        lifted = [jnp.exp2(s * EXP2_SCALE - top) for s in scores]
        dprobs = [dot_last(value[...], grad) for value in values]
        total = sum(col_sum(p) for p in lifted)
        inverse = 1.0 / total
        delta = sum(col_sum(p * d) for p, d in zip(lifted, dprobs)) * inverse
        query_part = None
        for i, key_t in enumerate((k_t, kp_t, tk_t)):
            weights = lifted[i] * inverse
            dscore = (weights * (dprobs[i] - delta)).astype(BF16)
            dk = dot_plain(dscore, query)
            dv = dot_plain(weights.astype(BF16), grad)
            dk_parts[i] = dk if r == 0 else dk_parts[i] + dk
            dv_parts[i] = dv if r == 0 else dv_parts[i] + dv
            part = dot_plain(key_t, dscore)
            query_part = part if query_part is None else query_part + part
        dq[r : r + tile, :] = (query_part.T * SCALE).astype(BF16)
    dko[...] = (dko[...] + dk_parts[0]) * SCALE
    dvo[...] = dvo[...] + dv_parts[0]
    dkp[...] = (dk_parts[1] * SCALE).astype(BF16)
    dvp[...] = dv_parts[1].astype(BF16)
    dtk[...] = (dtk[...] + dk_parts[2]) * SCALE
    dtv[...] = dtv[...] + dv_parts[2]


def return_kernel(
    blocks, heads, dq, dko, dvo, dkp, dvp, dtq, dtk, dtv,
    out_q, out_k, out_v, out_tq, out_tk, out_tv,
    back, ready, part, part16, x_in, x_sum, x_sum16, z_in, hi_in, z_all, x_all,
    a2a_sems, own_sems, back_sems, x_sems, z_sems, hi_sems, zg_sems, xg_sems,
):
    at = Place(blocks, heads)
    rows = out_q.shape[0]
    wide = dq.shape[1]
    per_dev = wide // HEAD_DIM
    txt = dtq.shape[0]
    meet(
        [(at.b, at.head_peer(s)) for s in range(1, heads)]
        + [at.next(), at.prev()]
        + [at.along_z(s)[1] for s in range(1, at.n_z)]
        + [at.along_x(s)[1] for s in range(1, at.n_x)]
        + [at.along_hi(s) for s in range(1, at.n_hi)]
    )
    my_cols = pl.ds(at.c * wide, wide)

    def hand_out(i, src, dst):
        copies = []
        for s in range(1, heads):
            peer = at.head_peer(s)
            copies.append(
                remote(
                    src.at[pl.ds(peer * rows, rows), :],
                    dst.at[:, my_cols],
                    a2a_sems,
                    (i, s),
                    (at.b, peer),
                )
            )
        copies.append(
            pltpu.make_async_copy(
                src.at[pl.ds(at.c * rows, rows), :], dst.at[:, my_cols], own_sems.at[i]
            )
        )
        for copy in copies:
            copy.start()
        return copies

    returned = []
    for i, src in enumerate((dkp, dvp)):
        copy = remote(src, back.at[i], back_sems, (i,), at.prev())
        copy.start()
        returned.append(copy)
    out_copies = hand_out(0, dq, out_q)

    for i, src in enumerate((dtq, dtk, dtv)):
        for h in range(per_dev):
            piece = pl.ds((i * per_dev + h) * txt, txt)
            value = src[:, h * HEAD_DIM : (h + 1) * HEAD_DIM]
            part[piece, :] = value
            part16[piece, :] = value.astype(BF16)
    n_xr = part.shape[0] // at.n_x
    n_zr = n_xr // at.n_z
    copies = []
    for s in range(1, at.n_x):
        x, device = at.along_x(s)
        copies.append(
            remote(part16.at[pl.ds(x * n_xr, n_xr), :], x_in.at[s - 1], x_sems, (s,), device)
        )
        copies[-1].start()
    for copy in copies:
        copy.wait()
    value = part[pl.ds(at.x * n_xr, n_xr), :]
    for s in range(1, at.n_x):
        value = value + x_in[s - 1].astype(F32)
    x_sum[...] = value
    x_sum16[...] = value.astype(BF16)
    copies = []
    for s in range(1, at.n_z):
        z, device = at.along_z(s)
        copies.append(
            remote(x_sum16.at[pl.ds(z * n_zr, n_zr), :], z_in.at[s - 1], z_sems, (s,), device)
        )
        copies[-1].start()

    for i, (src, dst) in enumerate(((dko, out_k), (dvo, out_v))):
        returned[i].wait()
        ready[i] = (src[...] + back[i].astype(F32)).astype(BF16)
        out_copies += hand_out(i + 1, ready.at[i], dst)

    for copy in copies:
        copy.wait()
    value = x_sum[pl.ds(at.z * n_zr, n_zr), :]
    for s in range(1, at.n_z):
        value = value + z_in[s - 1].astype(F32)
    hi_in[0] = value
    for s in range(1, at.n_hi):
        copy = remote(hi_in.at[0], hi_in.at[s], hi_sems, (s,), at.along_hi(s))
        copy.start()
        copy.wait()
        value = value + hi_in[s]
    mine = pl.ds(at.z * n_zr, n_zr)
    z_all[mine, :] = value.astype(BF16)
    copies = []
    for s in range(1, at.n_z):
        copies.append(
            remote(z_all.at[mine, :], z_all.at[mine, :], zg_sems, (s,), at.along_z(s)[1])
        )
        copies[-1].start()
    for copy in copies:
        copy.wait()
    mine = pl.ds(at.x * n_xr, n_xr)
    x_all[mine, :] = z_all[...]
    copies = []
    for s in range(1, at.n_x):
        copies.append(
            remote(z_all, x_all.at[mine, :], xg_sems, (s,), at.along_x(s)[1])
        )
        copies[-1].start()
    for copy in copies:
        copy.wait()
    for i, dst in enumerate((out_tq, out_tk, out_tv)):
        for h in range(per_dev):
            piece = pl.ds((i * per_dev + h) * txt, txt)
            dst[:, h * HEAD_DIM : (h + 1) * HEAD_DIM] = x_all[piece, :].astype(F32)
    for copy in out_copies:
        copy.wait()


def dma(*shape):
    return pltpu.SemaphoreType.DMA(shape)


def body(blocks, heads, img_q, img_k, img_v, img_g, txt_q, txt_k, txt_v, txt_g):
    n_hi, n_x, n_z = torus_sizes(blocks)
    rows, width = img_q.shape
    txt, wide = txt_q.shape
    block_rows = rows * heads
    per_dev = wide // HEAD_DIM
    in_vmem = pl.BlockSpec(memory_space=pltpu.VMEM)
    anywhere = pl.BlockSpec(memory_space=pl.ANY)
    block16 = jax.ShapeDtypeStruct((block_rows, wide), BF16)
    block32 = jax.ShapeDtypeStruct((block_rows, wide), F32)
    stat_shape = (3 * STAT_ROWS, txt)
    gathered = pl.pallas_call(
        functools.partial(gather_kernel, blocks, heads),
        out_shape=[block16] * 6 + [jax.ShapeDtypeStruct(stat_shape, F32)],
        in_specs=[anywhere] * 4 + [in_vmem] * 4,
        out_specs=[in_vmem] * 7,
        scratch_shapes=[
            pltpu.VMEM((n_z,) + stat_shape, F32),
            pltpu.VMEM((n_hi * n_x,) + stat_shape, F32),
            dma(2, 4, heads),
            dma(4),
            dma(2, 2),
            dma(2, n_z),
            dma(2, n_hi * n_x),
        ],
        compiler_params=pltpu.CompilerParams(
            collective_id=0, has_side_effects=True, vmem_limit_bytes=VMEM_LIMIT
        ),
        name="gather_rows",
    )(img_q, img_k, img_v, img_g, txt_q, txt_k, txt_v, txt_g)
    block_spec = pl.BlockSpec((block_rows, HEAD_DIM), lambda h: (0, h))
    text_spec = pl.BlockSpec((txt, HEAD_DIM), lambda h: (0, h))
    text32 = jax.ShapeDtypeStruct((txt, wide), F32)
    grads = pl.pallas_call(
        functools.partial(attention_kernel, blocks),
        grid=(per_dev,),
        out_shape=[block16, block32, block32, block16, block16] + [text32] * 3,
        in_specs=[block_spec] * 6
        + [text_spec] * 4
        + [pl.BlockSpec(stat_shape, lambda h: (0, 0))],
        out_specs=[block_spec] * 5 + [text_spec] * 3,
        compiler_params=pltpu.CompilerParams(vmem_limit_bytes=VMEM_LIMIT),
        name="attention_grads",
    )(*gathered[:6], txt_q, txt_k, txt_v, txt_g, gathered[6])
    n_rows = 3 * per_dev * txt
    x_rows = n_rows // n_x
    z_rows = x_rows // n_z
    out16 = jax.ShapeDtypeStruct((rows, width), BF16)
    return tuple(
        pl.pallas_call(
            functools.partial(return_kernel, blocks, heads),
            out_shape=[out16] * 3 + [text32] * 3,
            in_specs=[in_vmem] * 8,
            out_specs=[anywhere] * 3 + [in_vmem] * 3,
            scratch_shapes=[
                pltpu.VMEM((2, block_rows, wide), BF16),
                pltpu.VMEM((2, block_rows, wide), BF16),
                pltpu.VMEM((n_rows, HEAD_DIM), F32),
                pltpu.VMEM((n_rows, HEAD_DIM), BF16),
                pltpu.VMEM((n_x - 1, x_rows, HEAD_DIM), BF16),
                pltpu.VMEM((x_rows, HEAD_DIM), F32),
                pltpu.VMEM((x_rows, HEAD_DIM), BF16),
                pltpu.VMEM((n_z - 1, z_rows, HEAD_DIM), BF16),
                pltpu.VMEM((n_hi, z_rows, HEAD_DIM), F32),
                pltpu.VMEM((x_rows, HEAD_DIM), BF16),
                pltpu.VMEM((n_rows, HEAD_DIM), BF16),
                dma(2, 3, heads),
                dma(3),
                dma(2, 2),
                dma(2, n_x),
                dma(2, n_z),
                dma(2, n_hi),
                dma(2, n_z),
                dma(2, n_x),
            ],
            compiler_params=pltpu.CompilerParams(
                collective_id=1, has_side_effects=True, vmem_limit_bytes=VMEM_LIMIT
            ),
            name="return_rows",
        )(*grads)
    )


def solution(mesh):
    rows = P(("blk", "head"), None)
    text = P(None, "head")
    return jax.shard_map(
        functools.partial(body, mesh.shape["blk"], mesh.shape["head"]),
        mesh=mesh,
        in_specs=(rows,) * 4 + (text,) * 4,
        out_specs=(rows,) * 3 + (text,) * 3,
        check_vma=False,
    )
```

time: 1490 us -> 226 us (0.15)
  waiting for transfers between devices: 688 us -> 0 us
  blocking collectives: 556 us -> 0 us
  Pallas kernels: 0 us -> 209 us
  local copies, waits for them, and re-layouts: 101 us -> 14.5 us
  matrix products: 74.1 us -> 0 us
  starting transfers between devices: 38.4 us -> 0 us
    psum x1 -> x0, waiting for transfers between devices: 652 us -> none  [body(): lax.psum((heads_last(text_query_part), heads_last(text_key_part), heads_l...]
    psum x1 -> x0, blocking collectives: 352 us -> none  [body(): lax.psum((jnp.sum(lifted_text, axis=-1), jnp.sum(lifted_text * text_dprob...]
    pallas_call x0 -> x3, Pallas kernels: none -> 209 us  [the longest x1 97 us: body(): pl.pallas_call(functools.partial(return_kernel, blocks, heads), out_shape...]
    pmax x1 -> x0, blocking collectives: 204 us -> none  [body(): joint = lax.pmax(local_top, 'blk')]
    dot_general x40 -> x0, matrix products: 74.1 us -> none  [the longest x12 23.4 us: tall_dot(): lax.dot_general(left, right, (((0,), (0,)), ((), ())), preferred_element_...]
    all_to_all x7 -> x0, waiting for transfers between devices: 36.3 us -> none  [the longest x1 8.83 us: body(): lax.all_to_all(img_v, 'head', split_axis=1, concat_axis=0, tiled=True)]
    all_to_all x7 -> x0, starting transfers between devices: 34.5 us -> none  [the longest x1 5.81 us: body(): lax.all_to_all(image_value.astype(jnp.bfloat16), 'head', split_axis=0, co...]
    dynamic_update_slice x12 -> x0, local copies, waits for them, and re-layouts: 18.3 us -> none  [body(): lax.map(one_head, (query_heads, grad_heads, key_heads, value_heads, heads...]
  transfers between devices with their start and end apart: 12 -> 0, of which waited for: 6 -> 0; matrix products, arithmetic and copies ran while one was open for 5% -> 0% of each run, Pallas kernels for 0% -> 0%
where the time goes in v1:
time: 226 us; the launch traced here: 224 us
  Pallas kernels  209 us (92%)
  local copies, waits for them, and re-layouts  14.5 us (6%)
    pallas_call x1, Pallas kernels, body(): pl.pallas_call(functools.partial(return_kernel, blocks, heads), out_shape...  97 us
    pallas_call x1, Pallas kernels, body(): pl.pallas_call(functools.partial(gather_kernel, blocks, heads), out_shape...  88.2 us
    pallas_call x1, Pallas kernels, body(): pl.pallas_call(functools.partial(attention_kernel, blocks), grid=(per_dev...  23.6 us
    unnamed x28, local copies, waits for them, and re-layouts  14.5 us

profile of v1, /device:TPU:24, one launch (start us, length us, event | category | flops | bytes accessed | tf_op | source)
XLA Modules:
  0.0 224.0 jit_solution(11934887775280438486)
XLA Ops:
  0.6 0.0 copy-start
  0.6 1.0 copy-done
  1.6 0.0 copy-start.1
  1.6 1.0 copy-done.1
  2.6 0.0 copy-start.2
  2.6 1.0 copy-done.2
  3.6 0.0 copy-start.3
  3.6 1.0 copy-done.3
  4.6 88.2 %gather_rows.1 = (bf16[512,768]{1,0:T(8,128)(2,1)S(1)}, bf16[512,768]{1,0:T(8,128)(2,1)S(1)}, bf16[512,768]{1,0:T(8,128)(2,1)S(1)}, bf16[512,768]{1,0:T(8,128)(2...) custom-call(bf16[128,3072]{1,0:T(8,128)(2,1)} %img_q.1, bf16[128,3072]{1,0:T(8,128)(2,1)} %img_k.1, ...), custom_call_target="tpu_custom_call" | custom-call | tf_op jit(solution)/shard_map/gather_rows/pallas_call | solution.py:397
  92.8 0.0 copy-start.4
  92.8 0.9 copy-done.4
  93.7 0.0 copy-start.5
  93.7 0.9 copy-done.5
  94.6 0.0 copy-start.6
  94.6 0.9 copy-done.6
  95.5 23.6 %attention_grads.1 = (bf16[512,768]{1,0:T(8,128)(2,1)S(1)}, f32[512,768]{1,0:T(8,128)}, f32[512,768]{1,0:T(8,128)}, bf16[512,768]{1,0:T(8,128)(2,1)S(1)}, bf16[5...) custom-call(bf16[512,768]{1,0:T(8,128)(2,1)} %copy-done.4, ...), custom_call_target="tpu_custom_call" | custom-call | tf_op jit(solution)/shard_map/attention_grads/pallas_call | solution.py:419
  119.1 0.0 copy-start.7
  119.1 0.9 copy-done.7
  119.9 0.0 copy-start.8
  119.9 0.9 copy-done.8
  120.8 0.0 copy-start.9
  120.8 0.9 copy-done.9
  121.7 97.0 %return_rows.1 = (bf16[128,3072]{1,0:T(8,128)(2,1)S(1)}, bf16[128,3072]{1,0:T(8,128)(2,1)S(1)}, bf16[128,3072]{1,0:T(8,128)(2,1)S(1)}, f32[256,768]{1,0:T(8,128)...) custom-call(bf16[512,768]{1,0:T(8,128)(2,1)} %copy-done.7, f32[512,768]{1,0:T(8,128)} %get-tuple-element.29.dko, ...), custom_call_target="tpu_custom_call" | custom-call | tf_op jit(solution)/shard_map/return_rows/pallas_call | solution.py:435
  218.7 0.9 copy.20
  219.6 0.9 copy.21
  220.5 0.9 copy.22
  221.4 0.0 copy-start.10
  221.4 0.9 copy.23
  222.2 0.9 copy.24
  223.1 0.0 copy-done.10
  223.1 0.9 copy.25
Async XLA Ops:
  0.6 1.0 copy-start
  1.6 1.0 copy-start.1
  2.6 1.0 copy-start.2
  3.6 1.0 copy-start.3
  92.8 0.9 copy-start.4
  93.7 0.9 copy-start.5
  94.6 0.9 copy-start.6
  119.1 0.9 copy-start.7
  119.9 0.9 copy-start.8
  120.8 0.9 copy-start.9
  221.4 1.8 copy-start.10

commit v2 on v0

v2 whole, which is shorter than its diff:
```python
import functools
import math
from types import SimpleNamespace

import jax
import jax.numpy as jnp
from jax import lax
from jax.experimental import pallas as pl
from jax.experimental.pallas import tpu as pltpu
from jax.sharding import PartitionSpec as P

HEAD_DIM = 128
SCALE = HEAD_DIM ** (-0.5)
EXP2_SCALE = SCALE * math.log2(math.e)
MESH = pl.DeviceIdType.MESH
F32 = jnp.float32
BF16 = jnp.bfloat16
STAT_ROWS = 8
GROUP = 2
LEAD = 3
TILE = 256
VMEM_LIMIT = 50 * 1024 * 1024


def torus_sizes(blocks):
    return {64: (2, 4, 8), 8: (2, 2, 2), 4: (1, 2, 2)}[blocks]


class Place:
    def __init__(self, blocks, heads):
        self.blocks, self.heads = blocks, heads
        self.n_hi, self.n_x, self.n_z = torus_sizes(blocks)
        self.b = lax.axis_index("blk")
        self.c = lax.axis_index("head")
        self.z = lax.rem(self.b, self.n_z)
        self.x = lax.rem(self.b // self.n_z, self.n_x)
        self.hi = self.b // (self.n_z * self.n_x)

    def device(self, hi, x, z):
        return ((hi * self.n_x + x) * self.n_z + z, self.c)

    def next(self):
        return (lax.rem(self.b + 1, self.blocks), self.c)

    def prev(self):
        return (lax.rem(self.b + self.blocks - 1, self.blocks), self.c)

    def head_peer(self, step):
        return lax.rem(self.c + step, self.heads)

    def along_z(self, step):
        z = lax.rem(self.z + step, self.n_z)
        return z, self.device(self.hi, self.x, z)

    def along_x(self, step):
        x = lax.rem(self.x + step, self.n_x)
        return x, self.device(self.hi, x, self.z)

    def along_hi(self, step):
        return self.device(lax.rem(self.hi + step, self.n_hi), self.x, self.z)

    def in_plane(self, step):
        at = lax.rem(self.hi * self.n_x + self.x + step, self.n_hi * self.n_x)
        return self.device(at // self.n_x, lax.rem(at, self.n_x), self.z)


def meet(devices):
    barrier = pltpu.get_barrier_semaphore()
    for device in devices:
        pl.semaphore_signal(barrier, inc=1, device_id=device, device_id_type=MESH)
    pl.semaphore_wait(barrier, len(devices))


def remote(src, dst, sems, slot, device):
    return pltpu.make_async_remote_copy(
        src_ref=src,
        dst_ref=dst,
        send_sem=sems.at[(0,) + slot],
        recv_sem=sems.at[(1,) + slot],
        device_id=device,
        device_id_type=MESH,
    )


def dot_last(left, right):
    return lax.dot_general(
        left, right, (((1,), (1,)), ((), ())), preferred_element_type=F32
    )


def dot_plain(left, right):
    return lax.dot_general(
        left, right, (((1,), (0,)), ((), ())), preferred_element_type=F32
    )


def col_max(array):
    return jnp.max(array, axis=0, keepdims=True)


def col_sum(array):
    return jnp.sum(array, axis=0, keepdims=True)


def merge_stats(parts, per_group):
    rows = [[p[i * per_group : (i + 1) * per_group] for i in range(3)] for p in parts]
    top = functools.reduce(jnp.maximum, [r[0] for r in rows])
    total = jnp.zeros_like(top)
    dots = jnp.zeros_like(top)
    for part_top, part_total, part_dots in rows:
        factor = jnp.exp2(part_top - top)
        total += part_total * factor
        dots += part_dots * factor
    return top, total, dots


def dma(*shape):
    return pltpu.SemaphoreType.DMA(shape)


def scratch(blocks, heads, rows, wide, txt):
    n_hi, n_x, n_z = torus_sizes(blocks)
    plane = n_hi * n_x
    n = wide // HEAD_DIM
    groups = n // GROUP
    block = rows * heads
    sums = 3 * GROUP * txt
    xr = sums // n_x
    zr = xr // n_z
    d = HEAD_DIM
    return dict(
        text=pltpu.VMEM((4, txt, wide), BF16),
        landed=pltpu.VMEM((4, n, block, d), BF16),
        halo=pltpu.VMEM((2, n, block, d), BF16),
        ready=pltpu.VMEM((3, n, block, d), BF16),
        own=pltpu.VMEM((2, n, block, d), F32),
        give=pltpu.VMEM((2, n, block, d), BF16),
        back=pltpu.VMEM((2, n, block, d), BF16),
        stat_z=pltpu.VMEM((groups, n_z, STAT_ROWS, txt), F32),
        stat_p=pltpu.VMEM((groups, plane, STAT_ROWS, txt), F32),
        stat=pltpu.VMEM((groups, STAT_ROWS, txt), F32),
        part=pltpu.VMEM((groups, sums, d), F32),
        part16=pltpu.VMEM((groups, sums, d), BF16),
        x_in=pltpu.VMEM((groups, n_x - 1, xr, d), BF16),
        x_sum=pltpu.VMEM((groups, xr, d), F32),
        x_sum16=pltpu.VMEM((groups, xr, d), BF16),
        z_in=pltpu.VMEM((groups, n_z - 1, zr, d), BF16),
        hi_in=pltpu.VMEM((groups, n_hi, zr, d), F32),
        z_all=pltpu.VMEM((groups, xr, d), BF16),
        x_all=pltpu.VMEM((groups, sums, d), BF16),
        text_sems=dma(4),
        in_sems=dma(2, n, 4, heads),
        in_own=dma(n, 4),
        halo_sems=dma(2, n, 2),
        back_sems=dma(2, n, 2),
        out_sems=dma(2, n, 3, heads),
        out_own=dma(n, 3),
        sz_sems=dma(2, groups, n_z),
        sp_sems=dma(2, groups, plane),
        xs_sems=dma(2, groups, n_x),
        zs_sems=dma(2, groups, n_z),
        hi_sems=dma(2, groups, n_hi),
        zg_sems=dma(2, groups, n_z),
        xg_sems=dma(2, groups, n_x),
    )


def kernel(blocks, heads, names, *refs):
    ins, outs, rest = refs[:8], refs[8:14], refs[14:]
    images, texts = ins[:4], ins[4:]
    m = SimpleNamespace(**dict(zip(names, rest)))
    at = Place(blocks, heads)
    rows = outs[0].shape[0]
    txt, wide = outs[3].shape
    n = wide // HEAD_DIM
    groups = n // GROUP
    plane = at.n_hi * at.n_x
    xr, zr = m.x_sum.shape[1], m.z_in.shape[2]
    block = rows * heads
    my_rows = pl.ds(at.c * rows, rows)
    first = jnp.where(at.b == 0, 1.0, 0.0).astype(F32)

    def head_cols(owner, h):
        return pl.ds(pl.multiple_of(owner * wide + h * HEAD_DIM, HEAD_DIM), HEAD_DIM)


    def arrive(h, i, s):
        peer = at.head_peer(s)
        return remote(
            images[i].at[:, head_cols(peer, h)],
            m.landed.at[i, h, my_rows, :],
            m.in_sems, (h, i, s), (at.b, peer),
        )

    def arrive_own(h, i):
        return pltpu.make_async_copy(
            images[i].at[:, head_cols(at.c, h)],
            m.landed.at[i, h, my_rows, :],
            m.in_own.at[h, i],
        )

    def halo(h, i):
        return remote(
            m.landed.at[i + 1, h], m.halo.at[i, h], m.halo_sems, (h, i), at.next()
        )

    def give_back(h, i):
        return remote(m.give.at[i, h], m.back.at[i, h], m.back_sems, (h, i), at.prev())

    def leave(h, i, s):
        peer = at.head_peer(s)
        return remote(
            m.ready.at[i, h, pl.ds(peer * rows, rows), :],
            outs[i].at[:, head_cols(at.c, h)],
            m.out_sems, (h, i, s), (at.b, peer),
        )

    def leave_own(h, i):
        return pltpu.make_async_copy(
            m.ready.at[i, h, my_rows, :],
            outs[i].at[:, head_cols(at.c, h)],
            m.out_own.at[h, i],
        )

    def stats_z(g, s):
        return remote(
            m.stat_z.at[g, 0], m.stat_z.at[g, s], m.sz_sems, (g, s), at.along_z(s)[1]
        )

    def stats_p(g, s):
        return remote(
            m.stat_p.at[g, 0], m.stat_p.at[g, s], m.sp_sems, (g, s), at.in_plane(s)
        )

    def scatter_x(g, s):
        x, device = at.along_x(s)
        return remote(
            m.part16.at[g, pl.ds(x * xr, xr), :], m.x_in.at[g, s - 1],
            m.xs_sems, (g, s), device,
        )

    def scatter_z(g, s):
        z, device = at.along_z(s)
        return remote(
            m.x_sum16.at[g, pl.ds(z * zr, zr), :], m.z_in.at[g, s - 1],
            m.zs_sems, (g, s), device,
        )

    def swap_hi(g, s):
        return remote(
            m.hi_in.at[g, 0], m.hi_in.at[g, s], m.hi_sems, (g, s), at.along_hi(s)
        )

    my_z = pl.ds(at.z * zr, zr)
    my_x = pl.ds(at.x * xr, xr)

    def gather_z(g, s):
        return remote(
            m.z_all.at[g, my_z, :], m.z_all.at[g, my_z, :],
            m.zg_sems, (g, s), at.along_z(s)[1],
        )

    def gather_x(g, s):
        return remote(
            m.z_all.at[g], m.x_all.at[g, my_x, :],
            m.xg_sems, (g, s), at.along_x(s)[1],
        )

    group_moves = [
        (stats_z, at.n_z), (stats_p, plane), (scatter_x, at.n_x), (scatter_z, at.n_z),
        (swap_hi, at.n_hi), (gather_z, at.n_z), (gather_x, at.n_x),
    ]

    def start_all(move, count, g):
        for s in range(1, count):
            move(g, s).start()

    def await_all(move, count, g):
        for s in range(1, count):
            move(g, s).wait_recv()


    def send_in(h):
        for i in (1, 2, 0, 3):
            for s in (2, 3, 1) if heads == 4 else range(1, heads):
                arrive(h, i, s).start()
            arrive_own(h, i).start()

    def await_in(h, i):
        for s in range(1, heads):
            arrive(h, i, s).wait_recv()
        arrive_own(h, i).wait()

    def send_out(h, i):
        for s in (2, 3, 1) if heads == 4 else range(1, heads):
            leave(h, i, s).start()
        leave_own(h, i).start()

    def text_rows(i, h):
        return m.text[i, :, pl.ds(pl.multiple_of(h * HEAD_DIM, HEAD_DIM), HEAD_DIM)]

    def keys_in(h):
        for i in (1, 2):
            await_in(h, i)
            halo(h, i - 1).start()
        g, hh = h // GROUP, lax.rem(h, GROUP)
        query, grad = text_rows(0, h), text_rows(3, h)
        s_img = dot_last(m.landed[1, h], query) * EXP2_SCALE
        s_txt = dot_last(text_rows(1, h), query) * EXP2_SCALE
        top = jnp.maximum(col_max(s_img), col_max(s_txt))
        p_img = jnp.exp2(s_img - top)
        p_txt = jnp.exp2(s_txt - top) * first
        d_img = dot_last(m.landed[2, h], grad)
        d_txt = dot_last(text_rows(2, h), grad)
        m.stat_z[g, 0, pl.ds(hh, 1), :] = top
        m.stat_z[g, 0, pl.ds(GROUP + hh, 1), :] = col_sum(p_img) + col_sum(p_txt)
        m.stat_z[g, 0, pl.ds(2 * GROUP + hh, 1), :] = col_sum(p_img * d_img) + col_sum(
            p_txt * d_txt
        )

    def merge_z(g):
        await_all(stats_z, at.n_z, g)
        merged = merge_stats([m.stat_z[g, s] for s in range(at.n_z)], GROUP)
        m.stat_p[g, 0] = jnp.zeros_like(m.stat_p[g, 0])
        for i in range(3):
            m.stat_p[g, 0, i * GROUP : (i + 1) * GROUP, :] = merged[i]
        start_all(stats_p, plane, g)

    def merge_plane(g):
        await_all(stats_p, plane, g)
        merged = merge_stats([m.stat_p[g, s] for s in range(plane)], GROUP)
        for i in range(3):
            m.stat[g, i * GROUP : (i + 1) * GROUP, :] = merged[i]

    def part_rows(i, hh):
        return pl.ds(pl.multiple_of((i * GROUP + hh) * txt, txt), txt)

    def text_grads(g, hh):
        h = g * GROUP + hh
        query, grad = text_rows(0, h), text_rows(3, h)
        key, value = m.landed[1, h], m.landed[2, h]
        text_key, text_value = text_rows(1, h), text_rows(2, h)
        top = m.stat[g, pl.ds(hh, 1), :]
        total = m.stat[g, pl.ds(GROUP + hh, 1), :]
        inverse = 1.0 / total
        delta = m.stat[g, pl.ds(2 * GROUP + hh, 1), :] * inverse
        w_img = jnp.exp2(dot_last(key, query) * EXP2_SCALE - top) * inverse
        ds_img = (w_img * (dot_last(value, grad) - delta)).astype(BF16)
        w_txt = jnp.exp2(dot_last(text_key, query) * EXP2_SCALE - top) * (inverse * first)
        ds_txt = (w_txt * (dot_last(text_value, grad) - delta)).astype(BF16)
        m.own[0, h] += dot_plain(ds_img, query) * SCALE
        m.own[1, h] += dot_plain(w_img.astype(BF16), grad)
        sums = [
            (dot_plain(key.T, ds_img) + dot_plain(text_key.T, ds_txt)).T * SCALE,
            m.part[g, part_rows(1, hh), :] + dot_plain(ds_txt, query) * SCALE,
            m.part[g, part_rows(2, hh), :] + dot_plain(w_txt.astype(BF16), grad),
        ]
        for i in range(3):
            m.part[g, part_rows(i, hh), :] = sums[i]
            m.part16[g, part_rows(i, hh), :] = sums[i].astype(BF16)

    def image_grads(h):
        for i in (0, 3):
            await_in(h, i)
        for i in range(2):
            halo(h, i).wait_recv()
        g, hh = h // GROUP, lax.rem(h, GROUP)
        keys = [m.landed[1, h], m.halo[0, h], text_rows(1, h)]
        values = [m.landed[2, h], m.halo[1, h], text_rows(2, h)]
        turned = [key.T for key in keys]
        dk_parts, dv_parts = [None] * 3, [None] * 3
        for r in range(0, block, min(block, TILE)):
            these = slice(r, r + min(block, TILE))
            query, grad = m.landed[0, h, these, :], m.landed[3, h, these, :]
            scores = [dot_last(key, query) for key in keys]
            top = functools.reduce(jnp.maximum, [col_max(s) for s in scores]) * EXP2_SCALE
            lifted = [jnp.exp2(s * EXP2_SCALE - top) for s in scores]
            dprobs = [dot_last(value, grad) for value in values]
            inverse = 1.0 / sum(col_sum(p) for p in lifted)
            delta = sum(col_sum(p * d) for p, d in zip(lifted, dprobs)) * inverse
            query_part = None
            for i in range(3):
                weights = lifted[i] * inverse
                dscore = (weights * (dprobs[i] - delta)).astype(BF16)
                dk = dot_plain(dscore, query)
                dv = dot_plain(weights.astype(BF16), grad)
                dk_parts[i] = dk if r == 0 else dk_parts[i] + dk
                dv_parts[i] = dv if r == 0 else dv_parts[i] + dv
                part = dot_plain(turned[i], dscore)
                query_part = part if query_part is None else query_part + part
            m.ready[0, h, these, :] = (query_part.T * SCALE).astype(BF16)
        m.give[0, h] = (dk_parts[1] * SCALE).astype(BF16)
        m.give[1, h] = dv_parts[1].astype(BF16)
        for i in range(2):
            give_back(h, i).start()
        send_out(h, 0)
        m.own[0, h] = dk_parts[0] * SCALE
        m.own[1, h] = dv_parts[0]
        m.part[g, part_rows(1, hh), :] = dk_parts[2] * SCALE
        m.part[g, part_rows(2, hh), :] = dv_parts[2]

    def finish(h):
        for i in range(2):
            give_back(h, i).wait_recv()
            m.ready[i + 1, h] = (m.own[i, h] + m.back[i, h].astype(F32)).astype(BF16)
            send_out(h, i + 1)

    def sum_x(g):
        await_all(scatter_x, at.n_x, g)
        value = m.part[g, my_x, :]
        for s in range(1, at.n_x):
            value = value + m.x_in[g, s - 1].astype(F32)
        m.x_sum[g] = value
        m.x_sum16[g] = value.astype(BF16)
        start_all(scatter_z, at.n_z, g)

    def sum_z(g):
        await_all(scatter_z, at.n_z, g)
        value = m.x_sum[g, my_z, :]
        for s in range(1, at.n_z):
            value = value + m.z_in[g, s - 1].astype(F32)
        m.hi_in[g, 0] = value
        start_all(swap_hi, at.n_hi, g)

    def sum_hi(g):
        await_all(swap_hi, at.n_hi, g)
        value = m.hi_in[g, 0]
        for s in range(1, at.n_hi):
            value = value + m.hi_in[g, s]
        m.z_all[g, my_z, :] = value.astype(BF16)
        start_all(gather_z, at.n_z, g)

    def spread(g):
        await_all(gather_z, at.n_z, g)
        m.x_all[g, my_x, :] = m.z_all[g]
        start_all(gather_x, at.n_x, g)

    def write_text(g):
        await_all(gather_x, at.n_x, g)
        for i in range(3):
            for hh in range(GROUP):
                cols = pl.ds(pl.multiple_of((g * GROUP + hh) * HEAD_DIM, HEAD_DIM), HEAD_DIM)
                outs[3 + i][:, cols] = m.x_all[g, part_rows(i, hh), :].astype(F32)


    for g in range(groups):
        m.stat_z[g, 0] = jnp.zeros_like(m.stat_z[g, 0])
    meet(
        [(at.b, at.head_peer(s)) for s in range(1, heads)]
        + [at.next(), at.prev()]
        + [at.along_z(s)[1] for s in range(1, at.n_z)]
        + [at.in_plane(s) for s in range(1, plane)]
    )
    text_copies = [
        pltpu.make_async_copy(texts[i], m.text.at[i], m.text_sems.at[i]) for i in range(4)
    ]
    for copy in text_copies:
        copy.start()
    lead = min(LEAD, n)
    pl.loop(0, lead)(send_in)
    for copy in text_copies:
        copy.wait()

    def when_group(t, late, stage):
        past = t - late

        @pl.when((past >= 0) & (past < GROUP * groups) & (lax.rem(past + GROUP * groups, GROUP) == 0))
        def _():
            stage(past // GROUP)

    def when_head(t, late, stage):
        @pl.when((t >= late) & (t < n + late))
        def _():
            stage(t - late)

    def start_stats(g):
        start_all(stats_z, at.n_z, g)

    def late_text(g):
        merge_plane(g)
        pl.loop(0, GROUP)(functools.partial(text_grads, g))
        start_all(scatter_x, at.n_x, g)

    @pl.loop(0, GROUP * (groups - 1) + GROUP + 7)
    def turn(t):
        @pl.when(t + lead < n)
        def _():
            send_in(t + lead)

        when_head(t, 0, keys_in)
        when_group(t, GROUP - 1, start_stats)
        when_group(t, GROUP, merge_z)
        when_head(t, 1, image_grads)
        when_group(t, GROUP + 1, late_text)
        when_group(t, GROUP + 2, sum_x)
        when_head(t, GROUP + 1, finish)
        when_group(t, GROUP + 3, sum_z)
        when_group(t, GROUP + 4, sum_hi)
        when_group(t, GROUP + 5, spread)
        when_group(t, GROUP + 6, write_text)

    @pl.loop(0, n)
    def settle(h):
        for s in range(1, heads):
            for i in range(4):
                arrive(h, i, s).wait_send()
            for i in range(3):
                leave(h, i, s).wait()
        for i in range(3):
            leave_own(h, i).wait()
        for i in range(2):
            halo(h, i).wait_send()
            give_back(h, i).wait_send()

    @pl.loop(0, groups)
    def settle_groups(g):
        for move, count in group_moves:
            for s in range(1, count):
                move(g, s).wait_send()


def body(blocks, heads, img_q, img_k, img_v, img_g, txt_q, txt_k, txt_v, txt_g):
    rows, width = img_q.shape
    txt, wide = txt_q.shape
    in_vmem = pl.BlockSpec(memory_space=pltpu.VMEM)
    anywhere = pl.BlockSpec(memory_space=pltpu.HBM)
    buffers = scratch(blocks, heads, rows, wide, txt)
    out16 = jax.ShapeDtypeStruct((rows, width), BF16)
    text32 = jax.ShapeDtypeStruct((txt, wide), F32)
    return tuple(
        pl.pallas_call(
            functools.partial(kernel, blocks, heads, tuple(buffers)),
            out_shape=[out16] * 3 + [text32] * 3,
            in_specs=[anywhere] * 8,
            out_specs=[anywhere] * 3 + [in_vmem] * 3,
            scratch_shapes=list(buffers.values()),
            compiler_params=pltpu.CompilerParams(
                collective_id=0, has_side_effects=True, vmem_limit_bytes=VMEM_LIMIT
            ),
            name="joint_attention_grads",
        )(img_q, img_k, img_v, img_g, txt_q, txt_k, txt_v, txt_g)
    )


def solution(mesh):
    rows = P(("blk", "head"), None)
    text = P(None, "head")
    return jax.shard_map(
        functools.partial(body, mesh.shape["blk"], mesh.shape["head"]),
        mesh=mesh,
        in_specs=(rows,) * 4 + (text,) * 4,
        out_specs=(rows,) * 3 + (text,) * 3,
        check_vma=False,
    )
```

time: 1490 us -> 152 us (0.10)
  waiting for transfers between devices: 688 us -> 0 us
  blocking collectives: 556 us -> 0 us
  Pallas kernels: 0 us -> 139 us
  local copies, waits for them, and re-layouts: 101 us -> 10.9 us
  matrix products: 74.1 us -> 0 us
  starting transfers between devices: 38.4 us -> 0 us
    psum x1 -> x0, waiting for transfers between devices: 652 us -> none  [body(): lax.psum((heads_last(text_query_part), heads_last(text_key_part), heads_l...]
    psum x1 -> x0, blocking collectives: 352 us -> none  [body(): lax.psum((jnp.sum(lifted_text, axis=-1), jnp.sum(lifted_text * text_dprob...]
    pmax x1 -> x0, blocking collectives: 204 us -> none  [body(): joint = lax.pmax(local_top, 'blk')]
    pallas_call x0 -> x1, Pallas kernels: none -> 139 us  [body(): pl.pallas_call(functools.partial(kernel, blocks, heads, tuple(buffers)),...]
    dot_general x40 -> x0, matrix products: 74.1 us -> none  [the longest x12 23.4 us: tall_dot(): lax.dot_general(left, right, (((0,), (0,)), ((), ())), preferred_element_...]
    all_to_all x7 -> x0, waiting for transfers between devices: 36.3 us -> none  [the longest x1 8.83 us: body(): lax.all_to_all(img_v, 'head', split_axis=1, concat_axis=0, tiled=True)]
    all_to_all x7 -> x0, starting transfers between devices: 34.5 us -> none  [the longest x1 5.81 us: body(): lax.all_to_all(image_value.astype(jnp.bfloat16), 'head', split_axis=0, co...]
    dynamic_update_slice x12 -> x0, local copies, waits for them, and re-layouts: 18.3 us -> none  [body(): lax.map(one_head, (query_heads, grad_heads, key_heads, value_heads, heads...]
  transfers between devices with their start and end apart: 12 -> 0, of which waited for: 6 -> 0; matrix products, arithmetic and copies ran while one was open for 5% -> 0% of each run, Pallas kernels for 0% -> 0%
where the time goes in v2:
time: 152 us; the launch traced here: 150 us
  Pallas kernels  139 us (91%)
  local copies, waits for them, and re-layouts  10.9 us (7%)
    pallas_call x1, Pallas kernels, body(): pl.pallas_call(functools.partial(kernel, blocks, heads, tuple(buffers)),...  139 us
    unnamed x20, local copies, waits for them, and re-layouts  10.9 us

profile of v2, /device:TPU:24, one launch (start us, length us, event | category | flops | bytes accessed | tf_op | source)
XLA Modules:
  0.0 150.3 jit_solution(3175426835465830092)
XLA Ops:
  0.6 0.0 copy-start
  0.6 1.0 copy-done
  1.6 0.0 copy-start.1
  1.6 1.0 copy-done.1
  2.6 0.0 copy-start.2
  2.6 1.0 copy-done.2
  3.6 0.0 copy-start.3
  3.6 1.0 copy-done.3
  4.6 138.8 %joint_attention_grads.1 = (bf16[128,3072]{1,0:T(8,128)(2,1)S(1)}, bf16[128,3072]{1,0:T(8,128)(2,1)S(1)}, bf16[128,3072]{1,0:T(8,128)(2,1)S(1)}, f32[256,768]{1,...) custom-call(bf16[128,3072]{1,0:T(8,128)(2,1)} %refs_0_.1, bf16[128,3072]{1,0:T(8,128)(2,1)} %refs_1_.1, ...), custom_call_target="tpu_custom_call" | custom-call | tf_op jit(solution)/shard_map/joint_attention_grads/pallas_call | solution.py:531
  143.4 0.9 copy.20
  144.3 0.9 copy.21
  145.2 0.0 copy-start.6
  145.2 0.9 copy.22
  146.1 0.5 copy-done.6
  146.6 0.0 copy-start.5
  146.6 0.9 copy.23
  147.5 0.5 copy-done.5
  148.0 0.0 copy-start.4
  148.0 0.9 copy.24
  148.9 0.5 copy-done.4
  149.5 0.9 copy.25
Async XLA Ops:
  0.6 1.0 copy-start
  1.6 1.0 copy-start.1
  2.6 1.0 copy-start.2
  3.6 1.0 copy-start.3
  145.2 1.4 copy-start.6
  146.6 1.4 copy-start.5
  148.0 1.4 copy-start.4

commit v3 on v2

--- a/solution.py
+++ b/solution.py
@@ -17,13 +17,13 @@
 BF16 = jnp.bfloat16
 STAT_ROWS = 8
 GROUP = 2
-LEAD = 3
+LEAD = 2
 TILE = 256
 VMEM_LIMIT = 50 * 1024 * 1024
 
 
 def torus_sizes(blocks):
-    return {64: (2, 4, 8), 8: (2, 2, 2), 4: (1, 2, 2)}[blocks]
+    return {64: (2, 4, 8), 8: (2, 2, 2)}[blocks]
 
 
 class Place:
@@ -35,15 +35,23 @@
         self.z = lax.rem(self.b, self.n_z)
         self.x = lax.rem(self.b // self.n_z, self.n_x)
         self.hi = self.b // (self.n_z * self.n_x)
+        self.part = self.trade(self.hi, self.c)
+
+    def trade(self, hi, c):
+        return lax.rem(c + hi * (self.heads // 2), self.heads)
 
     def device(self, hi, x, z):
-        return ((hi * self.n_x + x) * self.n_z + z, self.c)
+        return ((hi * self.n_x + x) * self.n_z + z, self.trade(hi, self.part))
+
+    def shifted(self, by):
+        b = lax.rem(self.b + by + self.blocks, self.blocks)
+        return (b, self.trade(b // (self.n_z * self.n_x), self.part))
 
     def next(self):
-        return (lax.rem(self.b + 1, self.blocks), self.c)
+        return self.shifted(1)
 
     def prev(self):
-        return (lax.rem(self.b + self.blocks - 1, self.blocks), self.c)
+        return self.shifted(-1)
 
     def head_peer(self, step):
         return lax.rem(self.c + step, self.heads)
@@ -56,8 +64,11 @@
         x = lax.rem(self.x + step, self.n_x)
         return x, self.device(self.hi, x, self.z)
 
-    def along_hi(self, step):
-        return self.device(lax.rem(self.hi + step, self.n_hi), self.x, self.z)
+    def across(self):
+        return self.device(1 - self.hi, self.x, self.z)
+
+    def across_at(self, c):
+        return (((1 - self.hi) * self.n_x + self.x) * self.n_z + self.z, c)
 
     def in_plane(self, step):
         at = lax.rem(self.hi * self.n_x + self.x + step, self.n_hi * self.n_x)
@@ -129,7 +140,7 @@
     zr = xr // n_z
     d = HEAD_DIM
     return dict(
-        text=pltpu.VMEM((4, txt, wide), BF16),
+        text=pltpu.VMEM((4, n, txt, d), BF16),
         landed=pltpu.VMEM((4, n, block, d), BF16),
         halo=pltpu.VMEM((2, n, block, d), BF16),
         ready=pltpu.VMEM((3, n, block, d), BF16),
@@ -145,10 +156,11 @@
         x_sum=pltpu.VMEM((groups, xr, d), F32),
         x_sum16=pltpu.VMEM((groups, xr, d), BF16),
         z_in=pltpu.VMEM((groups, n_z - 1, zr, d), BF16),
-        hi_in=pltpu.VMEM((groups, n_hi, zr, d), F32),
+        hi_in=pltpu.VMEM((groups, 3, zr, d), F32),
         z_all=pltpu.VMEM((groups, xr, d), BF16),
         x_all=pltpu.VMEM((groups, sums, d), BF16),
-        text_sems=dma(4),
+        text_sems=dma(2, n, 4),
+        text_own=dma(n, 4),
         in_sems=dma(2, n, 4, heads),
         in_own=dma(n, 4),
         halo_sems=dma(2, n, 2),
@@ -159,7 +171,7 @@
         sp_sems=dma(2, groups, plane),
         xs_sems=dma(2, groups, n_x),
         zs_sems=dma(2, groups, n_z),
-        hi_sems=dma(2, groups, n_hi),
+        hi_sems=dma(2, groups, 3),
         zg_sems=dma(2, groups, n_z),
         xg_sems=dma(2, groups, n_x),
     )
@@ -179,6 +191,9 @@
     block = rows * heads
     my_rows = pl.ds(at.c * rows, rows)
     first = jnp.where(at.b == 0, 1.0, 0.0).astype(F32)
+    last_x, last_z = at.n_x - 1, at.n_z - 1
+    corner = ((at.x == 0) & (at.z == 0)) | ((at.x == last_x) & (at.z == last_z))
+    relays = ((1, 0, 0), (last_x - 1, last_z, last_x))
 
     def head_cols(owner, h):
         return pl.ds(pl.multiple_of(owner * wide + h * HEAD_DIM, HEAD_DIM), HEAD_DIM)
@@ -187,18 +202,33 @@
     def arrive(h, i, s):
         peer = at.head_peer(s)
         return remote(
-            images[i].at[:, head_cols(peer, h)],
+            images[i].at[:, head_cols(at.trade(at.hi, peer), h)],
             m.landed.at[i, h, my_rows, :],
             m.in_sems, (h, i, s), (at.b, peer),
         )
 
     def arrive_own(h, i):
         return pltpu.make_async_copy(
-            images[i].at[:, head_cols(at.c, h)],
+            images[i].at[:, head_cols(at.part, h)],
             m.landed.at[i, h, my_rows, :],
             m.in_own.at[h, i],
         )
 
+    def text_own(h, i):
+        return pltpu.make_async_copy(
+            texts[i].at[:, head_cols(0, h)], m.text.at[i, h], m.text_own.at[h, i]
+        )
+
+    def text_over(h, i):
+        return remote(
+            texts[i].at[:, head_cols(0, h)], m.text.at[i, h], m.text_sems, (h, i), at.across()
+        )
+
+    def text_relay(h, i, to_x):
+        return remote(
+            m.text.at[i, h], m.text.at[i, h], m.text_sems, (h, i), at.device(1, to_x, at.z)
+        )
+
     def halo(h, i):
         return remote(
             m.landed.at[i + 1, h], m.halo.at[i, h], m.halo_sems, (h, i), at.next()
@@ -211,14 +241,14 @@
         peer = at.head_peer(s)
         return remote(
             m.ready.at[i, h, pl.ds(peer * rows, rows), :],
-            outs[i].at[:, head_cols(at.c, h)],
+            outs[i].at[:, head_cols(at.part, h)],
             m.out_sems, (h, i, s), (at.b, peer),
         )
 
     def leave_own(h, i):
         return pltpu.make_async_copy(
             m.ready.at[i, h, my_rows, :],
-            outs[i].at[:, head_cols(at.c, h)],
+            outs[i].at[:, head_cols(at.part, h)],
             m.out_own.at[h, i],
         )
 
@@ -247,9 +277,8 @@
         )
 
     def swap_hi(g, s):
-        return remote(
-            m.hi_in.at[g, 0], m.hi_in.at[g, s], m.hi_sems, (g, s), at.along_hi(s)
-        )
+        device = at.across_at(at.part) if s == 1 else (at.b, at.part)
+        return remote(m.hi_in.at[g, 0], m.hi_in.at[g, s], m.hi_sems, (g, s), device)
 
     my_z = pl.ds(at.z * zr, zr)
     my_x = pl.ds(at.x * xr, xr)
@@ -268,7 +297,7 @@
 
     group_moves = [
         (stats_z, at.n_z), (stats_p, plane), (scatter_x, at.n_x), (scatter_z, at.n_z),
-        (swap_hi, at.n_hi), (gather_z, at.n_z), (gather_x, at.n_x),
+        (gather_z, at.n_z), (gather_x, at.n_x),
     ]
 
     def start_all(move, count, g):
@@ -280,11 +309,50 @@
             move(g, s).wait_recv()
 
 
-    def send_in(h):
-        for i in (1, 2, 0, 3):
+    def send_rows(h, arrays):
+        for i in arrays:
             for s in (2, 3, 1) if heads == 4 else range(1, heads):
                 arrive(h, i, s).start()
             arrive_own(h, i).start()
+
+    def send_in(h):
+        @pl.when(h == 0)
+        def _():
+            send_rows(h, (1, 2))
+
+        @pl.when(h < n - 1)
+        def _():
+            send_rows(h + 1, (1, 2))
+
+        send_rows(h, (0, 3))
+
+        @pl.when(at.hi == 0)
+        def _():
+            for i in (1, 0, 2, 3):
+                text_own(h, i).start()
+
+        @pl.when((at.hi == 0) & ~corner)
+        def _():
+            for i in (1, 0, 2, 3):
+                text_over(h, i).start()
+
+    def await_text(h):
+        @pl.when(at.hi == 0)
+        def _():
+            for i in range(4):
+                text_own(h, i).wait()
+
+        @pl.when(at.hi == 1)
+        def _():
+            for i in range(4):
+                text_over(h, i).wait_recv()
+
+        for x, z, to_x in relays:
+
+            @pl.when((at.hi == 1) & (at.z == z) & (at.x == x))
+            def _():
+                for i in range(4):
+                    text_relay(h, i, to_x).start()
 
     def await_in(h, i):
         for s in range(1, heads):
@@ -297,12 +365,15 @@
         leave_own(h, i).start()
 
     def text_rows(i, h):
-        return m.text[i, :, pl.ds(pl.multiple_of(h * HEAD_DIM, HEAD_DIM), HEAD_DIM)]
+        return m.text[i, h]
 
     def keys_in(h):
         for i in (1, 2):
             await_in(h, i)
             halo(h, i - 1).start()
+
+    def text_stats(h):
+        await_text(h)
         g, hh = h // GROUP, lax.rem(h, GROUP)
         query, grad = text_rows(0, h), text_rows(3, h)
         s_img = dot_last(m.landed[1, h], query) * EXP2_SCALE
@@ -420,14 +491,24 @@
         for s in range(1, at.n_z):
             value = value + m.z_in[g, s - 1].astype(F32)
         m.hi_in[g, 0] = value
-        start_all(swap_hi, at.n_hi, g)
+        swap_hi(g, 1).start()
+
+        @pl.when(at.hi == 1)
+        def _():
+            swap_hi(g, 2).start()
 
     def sum_hi(g):
-        await_all(swap_hi, at.n_hi, g)
-        value = m.hi_in[g, 0]
-        for s in range(1, at.n_hi):
-            value = value + m.hi_in[g, s]
-        m.z_all[g, my_z, :] = value.astype(BF16)
+        swap_hi(g, 1).wait_recv()
+
+        @pl.when(at.hi == 0)
+        def _():
+            m.z_all[g, my_z, :] = (m.hi_in[g, 0] + m.hi_in[g, 1]).astype(BF16)
+
+        @pl.when(at.hi == 1)
+        def _():
+            swap_hi(g, 2).wait_recv()
+            m.z_all[g, my_z, :] = (m.hi_in[g, 1] + m.hi_in[g, 2]).astype(BF16)
+
         start_all(gather_z, at.n_z, g)
 
     def spread(g):
@@ -447,26 +528,19 @@
         m.stat_z[g, 0] = jnp.zeros_like(m.stat_z[g, 0])
     meet(
         [(at.b, at.head_peer(s)) for s in range(1, heads)]
-        + [at.next(), at.prev()]
+        + [at.next(), at.prev(), at.across_at(at.c)]
         + [at.along_z(s)[1] for s in range(1, at.n_z)]
         + [at.in_plane(s) for s in range(1, plane)]
     )
-    text_copies = [
-        pltpu.make_async_copy(texts[i], m.text.at[i], m.text_sems.at[i]) for i in range(4)
-    ]
-    for copy in text_copies:
-        copy.start()
     lead = min(LEAD, n)
     pl.loop(0, lead)(send_in)
-    for copy in text_copies:
-        copy.wait()
-
-    def when_group(t, late, stage):
-        past = t - late
-
-        @pl.when((past >= 0) & (past < GROUP * groups) & (lax.rem(past + GROUP * groups, GROUP) == 0))
-        def _():
-            stage(past // GROUP)
+
+    last = groups - 1
+
+    def in_turn(t, when, stage, g):
+        @pl.when(t == when)
+        def _():
+            stage(g)
 
     def when_head(t, late, stage):
         @pl.when((t >= late) & (t < n + late))
@@ -481,23 +555,39 @@
         pl.loop(0, GROUP)(functools.partial(text_grads, g))
         start_all(scatter_x, at.n_x, g)
 
-    @pl.loop(0, GROUP * (groups - 1) + GROUP + 7)
+    train = [sum_x, sum_z, sum_hi, spread, write_text]
+
+    def text_train(t):
+        for g in range(groups):
+            for k, stage in enumerate(train):
+                in_turn(t, (n - 1 if g + 2 <= last and k == 0 else n + (g + 2 > last)) + k, stage, g)
+
+    @pl.loop(0, n + 6)
     def turn(t):
         @pl.when(t + lead < n)
         def _():
             send_in(t + lead)
 
         when_head(t, 0, keys_in)
-        when_group(t, GROUP - 1, start_stats)
-        when_group(t, GROUP, merge_z)
+        for g in range(groups):
+            in_turn(t, GROUP * g + (GROUP if g == last else GROUP + 1), merge_z, g)
         when_head(t, 1, image_grads)
-        when_group(t, GROUP + 1, late_text)
-        when_group(t, GROUP + 2, sum_x)
-        when_head(t, GROUP + 1, finish)
-        when_group(t, GROUP + 3, sum_z)
-        when_group(t, GROUP + 4, sum_hi)
-        when_group(t, GROUP + 5, spread)
-        when_group(t, GROUP + 6, write_text)
+        in_turn(t, n, late_text, last)
+        when_head(t, 0, text_stats)
+        for g in range(groups):
+            in_turn(t, GROUP * g + GROUP - 1, start_stats, g)
+        for g in range(last):
+            in_turn(t, GROUP * g + GROUP + 1, late_text, g)
+
+        @pl.when(t < n + GROUP)
+        def _():
+            when_head(t, GROUP + 1, finish)
+
+        text_train(t)
+
+        @pl.when(t >= n + GROUP)
+        def _():
+            when_head(t, GROUP + 1, finish)
 
     @pl.loop(0, n)
     def settle(h):
@@ -512,11 +602,28 @@
             halo(h, i).wait_send()
             give_back(h, i).wait_send()
 
+        @pl.when((at.hi == 0) & ~corner)
+        def _():
+            for i in range(4):
+                text_over(h, i).wait_send()
+
+        for x, z, to_x in relays:
+
+            @pl.when((at.hi == 1) & (at.z == z) & (at.x == x))
+            def _():
+                for i in range(4):
+                    text_relay(h, i, to_x).wait_send()
+
     @pl.loop(0, groups)
     def settle_groups(g):
         for move, count in group_moves:
             for s in range(1, count):
                 move(g, s).wait_send()
+        swap_hi(g, 1).wait_send()
+
+        @pl.when(at.hi == 1)
+        def _():
+            swap_hi(g, 2).wait_send()
 
 
 def body(blocks, heads, img_q, img_k, img_v, img_g, txt_q, txt_k, txt_v, txt_g):

time: 152 us -> 129 us (0.85)
  Pallas kernels: 139 us -> 117 us
    pallas_call x1, Pallas kernels: 139 us -> 117 us  [body(): pl.pallas_call(functools.partial(kernel, blocks, heads, tuple(buffers)),...]
where the time goes in v3:
time: 129 us
  Pallas kernels  117 us (91%)
  local copies, waits for them, and re-layouts  10.9 us (8%)
    pallas_call x1, Pallas kernels, body(): pl.pallas_call(functools.partial(kernel, blocks, heads, tuple(buffers)),...  117 us
    unnamed x20, local copies, waits for them, and re-layouts  10.9 us

profile of v3, /device:TPU:24, one launch (start us, length us, event | category | flops | bytes accessed | tf_op | source)
XLA Modules:
  0.0 128.7 jit_solution(2214793835182979300)
XLA Ops:
  0.6 0.0 copy-start
  0.6 1.0 copy-done
  1.6 0.0 copy-start.1
  1.6 1.0 copy-done.1
  2.6 0.0 copy-start.2
  2.6 1.0 copy-done.2
  3.6 0.0 copy-start.3
  3.6 1.0 copy-done.3
  4.6 117.1 %joint_attention_grads.1 = (bf16[128,3072]{1,0:T(8,128)(2,1)S(1)}, bf16[128,3072]{1,0:T(8,128)(2,1)S(1)}, bf16[128,3072]{1,0:T(8,128)(2,1)S(1)}, f32[256,768]{1,...) custom-call(bf16[128,3072]{1,0:T(8,128)(2,1)} %refs_0_.1, bf16[128,3072]{1,0:T(8,128)(2,1)} %refs_1_.1, ...), custom_call_target="tpu_custom_call" | custom-call | tf_op jit(solution)/shard_map/joint_attention_grads/pallas_call | solution.py:638
  121.8 0.9 copy.20
  122.6 0.9 copy.21
  123.5 0.0 copy-start.6
  123.5 0.9 copy.22
  124.4 0.5 copy-done.6
  124.9 0.0 copy-start.5
  124.9 0.9 copy.23
  125.8 0.5 copy-done.5
  126.4 0.0 copy-start.4
  126.4 0.9 copy.24
  127.2 0.5 copy-done.4
  127.8 0.9 copy.25
Async XLA Ops:
  0.6 1.0 copy-start
  1.6 1.0 copy-start.1
  2.6 1.0 copy-start.2
  3.6 1.0 copy-start.3
  123.5 1.4 %copy-start.6 = (f32[256,768]{1,0:T(8,128)S(1)}, f32[256,768]{1,0:T(8,128)}, u32[]{:S(2)}) copy-start(f32[256,768]{1,0:T(8,128)} %get-tuple-element.15) | copy-start | bytes 2359300
  124.9 1.4 %copy-start.5 = (f32[256,768]{1,0:T(8,128)S(1)}, f32[256,768]{1,0:T(8,128)}, u32[]{:S(2)}) copy-start(f32[256,768]{1,0:T(8,128)} %get-tuple-element.16) | copy-start | bytes 2359300
  126.4 1.4 %copy-start.4 = (f32[256,768]{1,0:T(8,128)S(1)}, f32[256,768]{1,0:T(8,128)}, u32[]{:S(2)}) copy-start(f32[256,768]{1,0:T(8,128)} %get-tuple-element.17) | copy-start | bytes 2359300

commit v4 on v3

--- a/solution.py
+++ b/solution.py
@@ -16,10 +16,10 @@
 F32 = jnp.float32
 BF16 = jnp.bfloat16
 STAT_ROWS = 8
-GROUP = 2
-LEAD = 2
+GROUPS = 3
+AHEAD = 3
 TILE = 256
-VMEM_LIMIT = 50 * 1024 * 1024
+VMEM_LIMIT = 62 * 1024 * 1024
 
 
 def torus_sizes(blocks):
@@ -113,8 +113,8 @@
     return jnp.sum(array, axis=0, keepdims=True)
 
 
-def merge_stats(parts, per_group):
-    rows = [[p[i * per_group : (i + 1) * per_group] for i in range(3)] for p in parts]
+def merge_stats(parts):
+    rows = [[p[i * STAT_ROWS : (i + 1) * STAT_ROWS] for i in range(3)] for p in parts]
     top = functools.reduce(jnp.maximum, [r[0] for r in rows])
     total = jnp.zeros_like(top)
     dots = jnp.zeros_like(top)
@@ -122,7 +122,7 @@
         factor = jnp.exp2(part_top - top)
         total += part_total * factor
         dots += part_dots * factor
-    return top, total, dots
+    return jnp.concatenate([top, total, dots], axis=0)
 
 
 def dma(*shape):
@@ -133,9 +133,9 @@
     n_hi, n_x, n_z = torus_sizes(blocks)
     plane = n_hi * n_x
     n = wide // HEAD_DIM
-    groups = n // GROUP
+    groups = GROUPS
     block = rows * heads
-    sums = 3 * GROUP * txt
+    sums = n * txt
     xr = sums // n_x
     zr = xr // n_z
     d = HEAD_DIM
@@ -147,11 +147,12 @@
         own=pltpu.VMEM((2, n, block, d), F32),
         give=pltpu.VMEM((2, n, block, d), BF16),
         back=pltpu.VMEM((2, n, block, d), BF16),
-        stat_z=pltpu.VMEM((groups, n_z, STAT_ROWS, txt), F32),
-        stat_p=pltpu.VMEM((groups, plane, STAT_ROWS, txt), F32),
-        stat=pltpu.VMEM((groups, STAT_ROWS, txt), F32),
+        stat_z=pltpu.VMEM((1, n_z, 3 * STAT_ROWS, txt), F32),
+        stat_p=pltpu.VMEM((1, plane, 3 * STAT_ROWS, txt), F32),
+        stat=pltpu.VMEM((3 * STAT_ROWS, txt), F32),
         part=pltpu.VMEM((groups, sums, d), F32),
         part16=pltpu.VMEM((groups, sums, d), BF16),
+        selfs=pltpu.VMEM((groups, sums, d), F32),
         x_in=pltpu.VMEM((groups, n_x - 1, xr, d), BF16),
         x_sum=pltpu.VMEM((groups, xr, d), F32),
         x_sum16=pltpu.VMEM((groups, xr, d), BF16),
@@ -167,8 +168,8 @@
         back_sems=dma(2, n, 2),
         out_sems=dma(2, n, 3, heads),
         out_own=dma(n, 3),
-        sz_sems=dma(2, groups, n_z),
-        sp_sems=dma(2, groups, plane),
+        sz_sems=dma(2, 1, n_z),
+        sp_sems=dma(2, 1, plane),
         xs_sems=dma(2, groups, n_x),
         zs_sems=dma(2, groups, n_z),
         hi_sems=dma(2, groups, 3),
@@ -185,12 +186,13 @@
     rows = outs[0].shape[0]
     txt, wide = outs[3].shape
     n = wide // HEAD_DIM
-    groups = n // GROUP
+    groups = GROUPS
+    per = n // 2
     plane = at.n_hi * at.n_x
     xr, zr = m.x_sum.shape[1], m.z_in.shape[2]
     block = rows * heads
     my_rows = pl.ds(at.c * rows, rows)
-    first = jnp.where(at.b == 0, 1.0, 0.0).astype(F32)
+    once = jnp.where(at.hi == 0, 1.0, 0.0).astype(F32)
     last_x, last_z = at.n_x - 1, at.n_z - 1
     corner = ((at.x == 0) & (at.z == 0)) | ((at.x == last_x) & (at.z == last_z))
     relays = ((1, 0, 0), (last_x - 1, last_z, last_x))
@@ -296,7 +298,7 @@
         )
 
     group_moves = [
-        (stats_z, at.n_z), (stats_p, plane), (scatter_x, at.n_x), (scatter_z, at.n_z),
+        (scatter_x, at.n_x), (scatter_z, at.n_z),
         (gather_z, at.n_z), (gather_x, at.n_x),
     ]
 
@@ -315,44 +317,43 @@
                 arrive(h, i, s).start()
             arrive_own(h, i).start()
 
-    def send_in(h):
-        @pl.when(h == 0)
-        def _():
-            send_rows(h, (1, 2))
-
-        @pl.when(h < n - 1)
-        def _():
-            send_rows(h + 1, (1, 2))
-
+    def send_keys(h):
+        send_rows(h, (1, 2))
+        send_text(h, (0, 3))
+
+        @pl.when(at.hi == 0)
+        def _():
+            for i in range(4):
+                text_own(h, i).start()
+
+    def send_queries(h):
         send_rows(h, (0, 3))
-
-        @pl.when(at.hi == 0)
-        def _():
-            for i in (1, 0, 2, 3):
-                text_own(h, i).start()
-
+        send_text(h, (1, 2))
+
+    def send_text(h, arrays):
         @pl.when((at.hi == 0) & ~corner)
         def _():
-            for i in (1, 0, 2, 3):
+            for i in arrays:
                 text_over(h, i).start()
 
-    def await_text(h):
+    def await_text(h, arrays):
+        @pl.when(at.hi == 1)
+        def _():
+            for i in arrays:
+                text_over(h, i).wait_recv()
+
+        for x, z, to_x in relays:
+
+            @pl.when((at.hi == 1) & (at.z == z) & (at.x == x))
+            def _():
+                for i in arrays:
+                    text_relay(h, i, to_x).start()
+
+    def await_text_own(h):
         @pl.when(at.hi == 0)
         def _():
             for i in range(4):
                 text_own(h, i).wait()
-
-        @pl.when(at.hi == 1)
-        def _():
-            for i in range(4):
-                text_over(h, i).wait_recv()
-
-        for x, z, to_x in relays:
-
-            @pl.when((at.hi == 1) & (at.z == z) & (at.x == x))
-            def _():
-                for i in range(4):
-                    text_relay(h, i, to_x).start()
 
     def await_in(h, i):
         for s in range(1, heads):
@@ -373,69 +374,75 @@
             halo(h, i - 1).start()
 
     def text_stats(h):
-        await_text(h)
-        g, hh = h // GROUP, lax.rem(h, GROUP)
+        await_text_own(h)
+        await_text(h, (0, 3))
         query, grad = text_rows(0, h), text_rows(3, h)
-        s_img = dot_last(m.landed[1, h], query) * EXP2_SCALE
-        s_txt = dot_last(text_rows(1, h), query) * EXP2_SCALE
-        top = jnp.maximum(col_max(s_img), col_max(s_txt))
-        p_img = jnp.exp2(s_img - top)
-        p_txt = jnp.exp2(s_txt - top) * first
-        d_img = dot_last(m.landed[2, h], grad)
-        d_txt = dot_last(text_rows(2, h), grad)
-        m.stat_z[g, 0, pl.ds(hh, 1), :] = top
-        m.stat_z[g, 0, pl.ds(GROUP + hh, 1), :] = col_sum(p_img) + col_sum(p_txt)
-        m.stat_z[g, 0, pl.ds(2 * GROUP + hh, 1), :] = col_sum(p_img * d_img) + col_sum(
-            p_txt * d_txt
-        )
-
-    def merge_z(g):
-        await_all(stats_z, at.n_z, g)
-        merged = merge_stats([m.stat_z[g, s] for s in range(at.n_z)], GROUP)
-        m.stat_p[g, 0] = jnp.zeros_like(m.stat_p[g, 0])
-        for i in range(3):
-            m.stat_p[g, 0, i * GROUP : (i + 1) * GROUP, :] = merged[i]
-        start_all(stats_p, plane, g)
-
-    def merge_plane(g):
-        await_all(stats_p, plane, g)
-        merged = merge_stats([m.stat_p[g, s] for s in range(plane)], GROUP)
-        for i in range(3):
-            m.stat[g, i * GROUP : (i + 1) * GROUP, :] = merged[i]
-
-    def part_rows(i, hh):
-        return pl.ds(pl.multiple_of((i * GROUP + hh) * txt, txt), txt)
-
-    def text_grads(g, hh):
-        h = g * GROUP + hh
+
+        def write(keys, values):
+            scores = [dot_last(key, query) * EXP2_SCALE for key in keys]
+            top = functools.reduce(jnp.maximum, [col_max(x) for x in scores])
+            lifted = [jnp.exp2(x - top) for x in scores]
+            dprobs = [dot_last(value, grad) for value in values]
+            m.stat_z[0, 0, pl.ds(h, 1), :] = top
+            m.stat_z[0, 0, pl.ds(STAT_ROWS + h, 1), :] = sum(col_sum(p) for p in lifted)
+            m.stat_z[0, 0, pl.ds(2 * STAT_ROWS + h, 1), :] = sum(
+                col_sum(p * d) for p, d in zip(lifted, dprobs)
+            )
+
+        @pl.when(at.b == 0)
+        def _():
+            write((m.landed[1, h], text_rows(1, h)), (m.landed[2, h], text_rows(2, h)))
+
+        @pl.when(at.b != 0)
+        def _():
+            write((m.landed[1, h],), (m.landed[2, h],))
+
+    def merge_z():
+        await_all(stats_z, at.n_z, 0)
+        m.stat_p[0, 0] = merge_stats([m.stat_z[0, s] for s in range(at.n_z)])
+        start_all(stats_p, plane, 0)
+
+    def merge_plane():
+        await_all(stats_p, plane, 0)
+        m.stat[...] = merge_stats([m.stat_p[0, s] for s in range(plane)])
+
+    def place(i, h):
+        if i == 0:
+            g, at_block = groups - 1, h
+        else:
+            g, at_block = h // per, 2 * lax.rem(h, per) + i - 1
+        return g, pl.ds(pl.multiple_of(at_block * txt, txt), txt)
+
+    def text_grads(h):
         query, grad = text_rows(0, h), text_rows(3, h)
         key, value = m.landed[1, h], m.landed[2, h]
         text_key, text_value = text_rows(1, h), text_rows(2, h)
-        top = m.stat[g, pl.ds(hh, 1), :]
-        total = m.stat[g, pl.ds(GROUP + hh, 1), :]
+        top = m.stat[pl.ds(h, 1), :]
+        total = m.stat[pl.ds(STAT_ROWS + h, 1), :]
         inverse = 1.0 / total
-        delta = m.stat[g, pl.ds(2 * GROUP + hh, 1), :] * inverse
+        delta = m.stat[pl.ds(2 * STAT_ROWS + h, 1), :] * inverse
         w_img = jnp.exp2(dot_last(key, query) * EXP2_SCALE - top) * inverse
         ds_img = (w_img * (dot_last(value, grad) - delta)).astype(BF16)
-        w_txt = jnp.exp2(dot_last(text_key, query) * EXP2_SCALE - top) * (inverse * first)
+        w_txt = jnp.exp2(dot_last(text_key, query) * EXP2_SCALE - top) * inverse
         ds_txt = (w_txt * (dot_last(text_value, grad) - delta)).astype(BF16)
         m.own[0, h] += dot_plain(ds_img, query) * SCALE
         m.own[1, h] += dot_plain(w_img.astype(BF16), grad)
-        sums = [
-            (dot_plain(key.T, ds_img) + dot_plain(text_key.T, ds_txt)).T * SCALE,
-            m.part[g, part_rows(1, hh), :] + dot_plain(ds_txt, query) * SCALE,
-            m.part[g, part_rows(2, hh), :] + dot_plain(w_txt.astype(BF16), grad),
-        ]
-        for i in range(3):
-            m.part[g, part_rows(i, hh), :] = sums[i]
-            m.part16[g, part_rows(i, hh), :] = sums[i].astype(BF16)
+        sums = dot_plain(key.T, ds_img).T * SCALE
+        g, where = place(0, h)
+        m.part[g, where, :] = sums
+        m.part16[g, where, :] = sums.astype(BF16)
+        m.selfs[g, where, :] = dot_plain(text_key.T, ds_txt).T * SCALE
+        g, where = place(1, h)
+        m.selfs[g, where, :] = dot_plain(ds_txt, query) * SCALE
+        g, where = place(2, h)
+        m.selfs[g, where, :] = dot_plain(w_txt.astype(BF16), grad)
 
     def image_grads(h):
+        await_text(h, (1, 2))
         for i in (0, 3):
             await_in(h, i)
         for i in range(2):
             halo(h, i).wait_recv()
-        g, hh = h // GROUP, lax.rem(h, GROUP)
         keys = [m.landed[1, h], m.halo[0, h], text_rows(1, h)]
         values = [m.landed[2, h], m.halo[1, h], text_rows(2, h)]
         turned = [key.T for key in keys]
@@ -467,8 +474,10 @@
         send_out(h, 0)
         m.own[0, h] = dk_parts[0] * SCALE
         m.own[1, h] = dv_parts[0]
-        m.part[g, part_rows(1, hh), :] = dk_parts[2] * SCALE
-        m.part[g, part_rows(2, hh), :] = dv_parts[2]
+        for i, sums in ((1, dk_parts[2] * SCALE), (2, dv_parts[2])):
+            g, where = place(i, h)
+            m.part[g, where, :] = sums
+            m.part16[g, where, :] = sums.astype(BF16)
 
     def finish(h):
         for i in range(2):
@@ -490,6 +499,7 @@
         value = m.x_sum[g, my_z, :]
         for s in range(1, at.n_z):
             value = value + m.z_in[g, s - 1].astype(F32)
+        value = value + m.selfs[g, pl.ds(at.x * xr + at.z * zr, zr), :] * once
         m.hi_in[g, 0] = value
         swap_hi(g, 1).start()
 
@@ -519,75 +529,87 @@
     def write_text(g):
         await_all(gather_x, at.n_x, g)
         for i in range(3):
-            for hh in range(GROUP):
-                cols = pl.ds(pl.multiple_of((g * GROUP + hh) * HEAD_DIM, HEAD_DIM), HEAD_DIM)
-                outs[3 + i][:, cols] = m.x_all[g, part_rows(i, hh), :].astype(F32)
-
-
-    for g in range(groups):
-        m.stat_z[g, 0] = jnp.zeros_like(m.stat_z[g, 0])
+            for h in range(n):
+                if (groups - 1 if i == 0 else h // per) == g:
+                    block_at = (h if i == 0 else 2 * (h % per) + i - 1) * txt
+                    outs[3 + i][:, h * HEAD_DIM : (h + 1) * HEAD_DIM] = m.x_all[
+                        g, block_at : block_at + txt, :
+                    ]
+
+
+    m.stat_z[0, 0] = jnp.zeros_like(m.stat_z[0, 0])
     meet(
         [(at.b, at.head_peer(s)) for s in range(1, heads)]
         + [at.next(), at.prev(), at.across_at(at.c)]
         + [at.along_z(s)[1] for s in range(1, at.n_z)]
         + [at.in_plane(s) for s in range(1, plane)]
     )
-    lead = min(LEAD, n)
-    pl.loop(0, lead)(send_in)
-
-    last = groups - 1
-
-    def in_turn(t, when, stage, g):
+    ahead = min(AHEAD, n - 2)
+    pl.loop(0, ahead)(send_keys)
+
+    @pl.loop(0, n)
+    def send(h):
+        send_queries(h)
+
+        @pl.when(h + ahead < n)
+        def _():
+            send_keys(h + ahead)
+
+    @pl.loop(0, ahead)
+    def begin(h):
+        keys_in(h)
+        text_stats(h)
+
+    def in_turn(t, when, stage, *args):
         @pl.when(t == when)
         def _():
-            stage(g)
-
-    def when_head(t, late, stage):
-        @pl.when((t >= late) & (t < n + late))
-        def _():
-            stage(t - late)
-
-    def start_stats(g):
-        start_all(stats_z, at.n_z, g)
-
-    def late_text(g):
-        merge_plane(g)
-        pl.loop(0, GROUP)(functools.partial(text_grads, g))
+            stage(*args)
+
+    def start_stats():
+        start_all(stats_z, at.n_z, 0)
+
+    def start_sums(g):
         start_all(scatter_x, at.n_x, g)
 
+    def late_text():
+        merge_plane()
+
+        @pl.loop(0, n)
+        def each(h):
+            text_grads(h)
+
+            @pl.when(h < n - 2)
+            def _():
+                finish(h)
+
+        start_sums(groups - 1)
+
     train = [sum_x, sum_z, sum_hi, spread, write_text]
-
-    def text_train(t):
-        for g in range(groups):
-            for k, stage in enumerate(train):
-                in_turn(t, (n - 1 if g + 2 <= last and k == 0 else n + (g + 2 > last)) + k, stage, g)
 
     @pl.loop(0, n + 6)
     def turn(t):
-        @pl.when(t + lead < n)
-        def _():
-            send_in(t + lead)
-
-        when_head(t, 0, keys_in)
-        for g in range(groups):
-            in_turn(t, GROUP * g + (GROUP if g == last else GROUP + 1), merge_z, g)
-        when_head(t, 1, image_grads)
-        in_turn(t, n, late_text, last)
-        when_head(t, 0, text_stats)
-        for g in range(groups):
-            in_turn(t, GROUP * g + GROUP - 1, start_stats, g)
-        for g in range(last):
-            in_turn(t, GROUP * g + GROUP + 1, late_text, g)
-
-        @pl.when(t < n + GROUP)
-        def _():
-            when_head(t, GROUP + 1, finish)
-
-        text_train(t)
-
-        @pl.when(t >= n + GROUP)
-        def _():
-            when_head(t, GROUP + 1, finish)
+        @pl.when(t < n)
+        def _():
+            image_grads(t)
+
+        in_turn(t, per - 1, start_sums, 0)
+        in_turn(t, n - 1, start_sums, 1)
+
+        @pl.when(t + ahead < n)
+        def _():
+            keys_in(t + ahead)
+            text_stats(t + ahead)
+
+        in_turn(t, n - ahead - 1, start_stats)
+        in_turn(t, n - 2, merge_z)
+        in_turn(t, n - 1, late_text)
+        in_turn(t, n - 2, sum_x, 0)
+        in_turn(t, n, finish, n - 2)
+        for k, stage in enumerate(train):
+            for g in reversed(range(groups)):
+                if k or g:
+                    in_turn(t, n - 1 + k + g, stage, g)
+        in_turn(t, n + 1, finish, n - 1)
 
     @pl.loop(0, n)
     def settle(h):
@@ -614,6 +636,10 @@
                 for i in range(4):
                     text_relay(h, i, to_x).wait_send()
 
+    for move, count in ((stats_z, at.n_z), (stats_p, plane)):
+        for s in range(1, count):
+            move(0, s).wait_send()
+
     @pl.loop(0, groups)
     def settle_groups(g):
         for move, count in group_moves:
@@ -633,20 +659,19 @@
     anywhere = pl.BlockSpec(memory_space=pltpu.HBM)
     buffers = scratch(blocks, heads, rows, wide, txt)
     out16 = jax.ShapeDtypeStruct((rows, width), BF16)
-    text32 = jax.ShapeDtypeStruct((txt, wide), F32)
-    return tuple(
-        pl.pallas_call(
-            functools.partial(kernel, blocks, heads, tuple(buffers)),
-            out_shape=[out16] * 3 + [text32] * 3,
-            in_specs=[anywhere] * 8,
-            out_specs=[anywhere] * 3 + [in_vmem] * 3,
-            scratch_shapes=list(buffers.values()),
-            compiler_params=pltpu.CompilerParams(
-                collective_id=0, has_side_effects=True, vmem_limit_bytes=VMEM_LIMIT
-            ),
-            name="joint_attention_grads",
-        )(img_q, img_k, img_v, img_g, txt_q, txt_k, txt_v, txt_g)
-    )
+    text16 = jax.ShapeDtypeStruct((txt, wide), BF16)
+    grads = pl.pallas_call(
+        functools.partial(kernel, blocks, heads, tuple(buffers)),
+        out_shape=[out16] * 3 + [text16] * 3,
+        in_specs=[anywhere] * 8,
+        out_specs=[anywhere] * 3 + [in_vmem] * 3,
+        scratch_shapes=list(buffers.values()),
+        compiler_params=pltpu.CompilerParams(
+            collective_id=0, has_side_effects=True, vmem_limit_bytes=VMEM_LIMIT
+        ),
+        name="joint_attention_grads",
+    )(img_q, img_k, img_v, img_g, txt_q, txt_k, txt_v, txt_g)
+    return (*grads[:3], *(total.astype(F32) for total in grads[3:]))
 
 
 def solution(mesh):

time: 129 us -> 121 us (0.938)
  local copies, waits for them, and re-layouts: 10.9 us -> 4.38 us
  Pallas kernels: 117 us -> 112 us
  other arithmetic: 0 us -> 3.84 us
    unnamed x20 -> x13, local copies, waits for them, and re-layouts: 10.9 us -> 4.38 us
    pallas_call x1, Pallas kernels: 117 us -> 112 us  [body(): pl.pallas_call(functools.partial(kernel, blocks, heads, tuple(buffers)),...]
    convert_element_type x0 -> x3, other arithmetic: none -> 3.84 us  [body(): return (*grads[:3], *(total.astype(F32) for total in grads[3:]))]
where the time goes in v4:
time: 121 us
  Pallas kernels  112 us (93%)
  local copies, waits for them, and re-layouts  4.38 us (4%)
  other arithmetic  3.84 us (3%)
    pallas_call x1, Pallas kernels, body(): pl.pallas_call(functools.partial(kernel, blocks, heads, tuple(buffers)),...  112 us
    unnamed x13, local copies, waits for them, and re-layouts  4.38 us
    convert_element_type x3, other arithmetic, body(): return (*grads[:3], *(total.astype(F32) for total in grads[3:]))  3.84 us

profile of v4, /device:TPU:24, one launch (start us, length us, event | category | flops | bytes accessed | tf_op | source)
XLA Modules:
  0.0 120.6 jit_solution(10757114435886860223)
XLA Ops:
  0.6 111.7 %joint_attention_grads.1 = (bf16[128,3072]{1,0:T(8,128)(2,1)}, bf16[128,3072]{1,0:T(8,128)(2,1)}, bf16[128,3072]{1,0:T(8,128)(2,1)}, bf16[256,768]{1,0:T(8,128)(...) custom-call(bf16[128,3072]{1,0:T(8,128)(2,1)} %refs_0_.1, bf16[128,3072]{1,0:T(8,128)(2,1)} %refs_1_.1, ...), custom_call_target="tpu_custom_call" | custom-call | tf_op jit(solution)/shard_map/joint_attention_grads/pallas_call | solution.py:663
  112.3 0.0 copy-start.4
  112.3 2.0 %convert_element_type.9 = f32[256,768]{1,0:T(8,128)} convert(bf16[256,768]{1,0:T(8,128)(2,1)} %get-tuple-element.15) | non-fusion elementwise | flops 196608 | bytes 1179648 | tf_op jit(solution)/shard_map/convert_element_type | solution.py:674
  114.3 0.0 copy-done.4
  114.3 0.0 copy-start.3
  114.3 0.9 convert_element_type.10
  115.3 0.2 copy-done.3
  115.4 0.0 copy-start.2
  115.4 0.9 convert_element_type.11
  116.4 0.5 copy-done.2
  116.9 0.0 copy-start.1
  116.9 0.9 copy.17
  117.7 0.5 copy-done.1
  118.3 0.0 copy-start
  118.3 0.9 copy.18
  119.2 0.5 copy-done
  119.7 0.9 copy.19
Async XLA Ops:
  112.3 2.0 %copy-start.4 = (bf16[256,768]{1,0:T(8,128)(2,1)S(1)}, bf16[256,768]{1,0:T(8,128)(2,1)}, u32[]{:S(2)}) copy-start(bf16[256,768]{1,0:T(8,128)(2,1)} %get-tuple-element.16) | copy-start | bytes 1179652
  114.3 1.1 copy-start.3
  115.4 1.4 %copy-start.2 = (bf16[128,3072]{1,0:T(8,128)(2,1)S(1)}, bf16[128,3072]{1,0:T(8,128)(2,1)}, u32[]{:S(2)}) copy-start(bf16[128,3072]{1,0:T(8,128)(2,1)} %get-tuple-element.24) | copy-start | bytes 2359300
  116.9 1.4 %copy-start.1 = (bf16[128,3072]{1,0:T(8,128)(2,1)S(1)}, bf16[128,3072]{1,0:T(8,128)(2,1)}, u32[]{:S(2)}) copy-start(bf16[128,3072]{1,0:T(8,128)(2,1)} %get-tuple-element.25) | copy-start | bytes 2359300
  118.3 1.4 %copy-start = (bf16[128,3072]{1,0:T(8,128)(2,1)S(1)}, bf16[128,3072]{1,0:T(8,128)(2,1)}, u32[]{:S(2)}) copy-start(bf16[128,3072]{1,0:T(8,128)(2,1)} %get-tuple-element.26) | copy-start | bytes 2359300
